TPU v7x, 512 devices: a whole 4x4x16 slice. The times are simulated.
512 devices in a mesh: slab: 128 (over x, z, y_lo), row: 4 (over y_hi, core).
Axes of the slice: x: 4, y: 4 (y_hi: 2, y_lo: 2; y = y_hi * 2 + y_lo), z: 16, core: 2. Of those that a mesh axis runs over, the one named last changes fastest.
Arguments:
- image: bfloat16 [512, 128, 128], P('slab', 'row'), may hold values from -6 to 6
- first_kernel: bfloat16 [3, 3, 32, 1], replicated, may hold values from -2 to 2
- first_bias: float32 [32], replicated, may hold values from -1.5 to 1.5
- middle_kernel: bfloat16 [3, 3, 32, 32], replicated, may hold values from -0.5 to 0.5
- middle_bias: float32 [32], replicated, may hold values from -1.5 to 1.5
- last_kernel: bfloat16 [3, 3, 3, 32], replicated, may hold values from -0.5 to 0.5
- last_bias: float32 [3], replicated, may hold values from -2 to 2
Outputs:
- flows: float32 [4, 512, 128, 128], P(None, 'slab', 'row')
All inputs are finite; a program needn't handle non-finite values.
Results may differ from a plain program's by a relative error of at most 0.0052.
Values may be sent and summed in bfloat16 or wider, within the bound.
A program may use at most 64 MiB of HBM per device.

v0:
```python
import jax
import jax.numpy as jnp
from jax import lax
from jax.sharding import PartitionSpec as P


def with_halo(array, sides, width):
    for axis, dim in sides:
        devices, length = (lax.axis_size(axis), array.shape[dim])
        up = [(i, (i + 1) % devices) for i in range(devices - 1)]
        down = [(j, i) for i, j in up]
        last = lax.slice_in_dim(array, length - width, length, axis=dim)
        initial = lax.slice_in_dim(array, 0, width, axis=dim)
        before = lax.ppermute(last, axis, up)
        after = lax.ppermute(initial, axis, down)
        array = jnp.concatenate([before, array, after], axis=dim)
    return array


def flatten_kernel(kernel):
    outputs = kernel.shape[2]
    inputs = kernel.shape[3]
    return kernel.transpose(2, 0, 1, 3).reshape(outputs, 9 * inputs)


def apply_layer(values, kernel, bias):
    rows = values.shape[1] - 2
    cols = values.shape[2] - 2
    taps = []
    for row_shift in range(3):
        for col_shift in range(3):
            sliced = lax.slice_in_dim(values, row_shift, row_shift + rows, axis=1)
            taps.append(lax.slice_in_dim(sliced, col_shift, col_shift + cols, axis=2))
    stacked = jnp.concatenate(taps, axis=0)
    result = jnp.einsum("ok,k...->o...", kernel, stacked, preferred_element_type=jnp.float32)
    return result + bias.reshape((-1,) + (1,) * (values.ndim - 1))


def keep_inside(values, axis_pos, anchor, limit):
    coords = anchor + jnp.arange(values.shape[axis_pos], dtype=jnp.int32)
    inside = ((coords >= 0) & (coords < limit)).astype(values.dtype)
    shape = [1] * values.ndim
    shape[axis_pos] = values.shape[axis_pos]
    return values * inside.reshape(shape)


def forward(plane, kernels, biases, q_extended, q_anchor, q_total):
    rows_local = plane.shape[1]
    y_total = rows_local * lax.axis_size("row")
    y_anchor = lax.axis_index("row") * rows_local
    current = with_halo(plane, (("row", 1),), 3)
    y_anchor = y_anchor - 3
    for level_index in range(3):
        if not q_extended:
            padding = [(0, 0), (0, 0), (1, 1)] + [(0, 0)] * (current.ndim - 3)
            current = jnp.pad(current, padding)
        result = apply_layer(current, kernels[level_index], biases[level_index])
        if level_index == 2:
            return result
        result = jax.nn.relu(result)
        y_anchor = y_anchor + 1
        result = keep_inside(result, 1, y_anchor, y_total)
        if q_extended:
            q_anchor = q_anchor + 1
            result = keep_inside(result, 2, q_anchor, q_total)
        current = result.astype(jnp.bfloat16)
    return current


def local(image, first_kernel, first_bias, middle_kernel, middle_bias, last_kernel, last_bias):
    weights = (first_kernel, middle_kernel, last_kernel)
    biases = (first_bias, middle_bias, last_bias)
    kernels_xy = [flatten_kernel(weight) for weight in weights]
    kernels_yz = [flatten_kernel(weight.transpose(1, 0, 2, 3)) for weight in weights]
    depth_z = image.shape[0]
    total_z = depth_z * lax.axis_size("slab")
    xy_planes = image.transpose(1, 2, 0)[None]
    xy_flows = forward(xy_planes, kernels_xy, biases, False, 0, 0)
    xy_moved = xy_flows.transpose(0, 3, 1, 2)
    extended = with_halo(image, (("slab", 0),), 3)
    z_anchor = lax.axis_index("slab") * depth_z - 3
    yz_planes = extended.transpose(1, 0, 2)[None]
    yz_blocks = forward(yz_planes, kernels_yz, biases, True, z_anchor, total_z)
    yz_flows = yz_blocks.transpose(0, 2, 1, 3)
    return jnp.stack(
        [
            yz_flows[0],
            0.5 * (xy_moved[0] + yz_flows[1]),
            xy_moved[1],
            0.5 * (xy_moved[2] + yz_flows[2]),
        ]
    )


def solution(mesh):
    placed = (P("slab", "row", None), P(), P(), P(), P(), P(), P())
    return jax.shard_map(
        local, mesh=mesh, in_specs=placed, out_specs=P(None, "slab", "row", None), check_vma=False
    )
```

profile of v0, /device:TPU:7, one launch (start us, length us, event | category | flops | bytes accessed | tf_op | source)
XLA Modules:
  0.0 76.4 jit_solution(3150566490107067060)
XLA Ops:
  0.0 0.8 %fusion.29 = (bf16[3,32,128]{2,1,0:T(8,128)(2,1)S(1)}, bf16[3,32,128]{2,1,0:T(8,128)(2,1)S(1)}) fusion(bf16[4,32,128]{2,1,0:T(8,128)(2,1)} %param.7), kind=kLoop, calls=%fused_computation.91 | loop fusion | bytes 98304 | tf_op jit(solution)/shard_map/slice | solution.py:12
  0.8 12.4 %collective-permute-start.1 = (bf16[3,32,128]{2,1,0:T(8,128)(2,1)S(1)}, bf16[3,32,128]{2,1,0:T(8,128)(2,1)S(1)}, u32[]{:S(2)}, u32[]{:S(2)}) collective-permute-start(bf16[3,32,128]{2,1,0:T(8,128)(2,1)S(1)} %get-tuple-element.32), channel_id=1, source_target_pairs={{4,0},{8,4},{12,8},{16,12},{20,16},{24,20},{28,24},{32,28},{36,32}... | collective-permute-start | bytes 73736 | tf_op jit(solution)/shard_map/ppermute | solution.py:15
  13.2 1.9 %collective-permute-start = (bf16[3,32,128]{2,1,0:T(8,128)(2,1)S(1)}, bf16[3,32,128]{2,1,0:T(8,128)(2,1)S(1)}, u32[]{:S(2)}, u32[]{:S(2)}) collective-permute-start(bf16[3,32,128]{2,1,0:T(8,128)(2,1)S(1)} %get-tuple-element.31), channel_id=1, source_target_pairs={{0,4},{4,8},{8,12},{12,16},{16,20},{20,24},{24,28},{28,32},{32,36}... | collective-permute-start | bytes 73736 | tf_op jit(solution)/shard_map/ppermute | solution.py:14
  15.1 0.7 fusion.28
  15.9 5.4 %collective-permute-start.4 = (bf16[1,3,128,4]{2,0,3,1:T(2,128)(2,1)S(1)}, bf16[1,3,128,4]{2,0,3,1:T(2,128)(2,1)S(1)}, u32[]{:S(2)}, u32[]{:S(2)}) collective-permute-start(bf16[1,3,128,4]{2,0,3,1:T(2,128)(2,1)S(1)} %copy.35), channel_id=1, source_target_pairs={{0,1},{1,2},{2,3},{4,5},{5,6},{6,7},{8,9},{9,10},{10,11},{12,13},{... | collective-permute-start | bytes 9224 | tf_op jit(solution)/shard_map/ppermute | solution.py:14
  21.3 1.9 %collective-permute-start.5 = (bf16[1,3,128,4]{2,0,3,1:T(2,128)(2,1)S(1)}, bf16[1,3,128,4]{2,0,3,1:T(2,128)(2,1)S(1)}, u32[]{:S(2)}, u32[]{:S(2)}) collective-permute-start(bf16[1,3,128,4]{2,0,3,1:T(2,128)(2,1)S(1)} %copy.36), channel_id=1, source_target_pairs={{1,0},{2,1},{3,2},{5,4},{6,5},{7,6},{9,8},{10,9},{11,10},{13,12},{... | collective-permute-start | bytes 9224 | tf_op jit(solution)/shard_map/ppermute | solution.py:15
  23.3 0.7 copy.16
  24.0 0.9 %copy.17 = bf16[32,3,3,32]{3,2,1,0:T(4,128)(2,1)S(1)} copy(bf16[32,3,3,32]{3,0,1,2:T(8,128)(2,1)} %bitcast.55) | data formatting | bytes 36864 | tf_op jit(solution)/shard_map/transpose;transpose | solution.py:23
  25.0 0.7 copy.18
  25.8 0.7 reshape.74
  26.5 0.9 %copy.22 = bf16[32,3,3,32]{3,2,1,0:T(4,128)(2,1)S(1)} copy(bf16[32,3,3,32]{3,0,2,1:T(8,128)(2,1)} %bitcast.56) | data formatting | bytes 36864 | tf_op jit(solution)/shard_map/transpose | solution.py:23
  27.6 0.7 copy.23
  28.4 0.8 %constant_dynamic-update-slice_fusion.4 = bf16[1,38,128,4]{2,0,3,1:T(2,128)(2,1)S(1)} fusion(bf16[1,38,128,4]{2,0,3,1:T(2,128)(2,1)S(1)} %constant_dynamic-update-slice_fusion.5, bf16[1,32,128,4]{2,1,3,0:T(8,128)(2,1)} %bitcast.54), kind=kLoop, calls=%fused_computation.65 | loop fusion | bytes 98304
  29.2 0.8 %pad_slice_fusion.12 = (bf16[1,36,128,4]{2,0,3,1:T(2,128)(2,1)S(1)}, bf16[1,36,128,4]{2,0,3,1:T(2,128)(2,1)S(1)}, bf16[1,36,128,4]{2,0,3,1:T(2,128)(2,1)S(1)}, b...) fusion(bf16[1,38,128,4]{2,0,3,1:T(2,128)(2,1)S(1)} %constant_dy, ...), kind=kLoop, calls=%fused_computation.82 | loop fusion | bytes 630784 | tf_op jit(solution)/shard_map/slice | solution.py:33
  30.1 1.2 %concatenate.33 = bf16[9,36,128,4]{2,0,3,1:T(8,128)(2,1)S(1)} concatenate(bf16[1,36,128,4]{2,0,3,1:T(2,128)(2,1)S(1)} %get-tuple-element.28, bf16[1,36,128,4]{2,0,3,1:T(2,128)(2,1)S(1)} %get-tuple-element.27, bf16[1,36,128,4]{2,0,3,1:T(2,128)(2,1)S(1)} %get-tuple-element.21, bf16[1,36,128,4]{2,0,3,1:T(2,128)(2,1)S(1)} %get-tuple-element.22, ...), dimensions={0} | concatenate | bytes 663552 | tf_op jit(solution)/shard_map/concatenate | solution.py:34
  31.3 1.2 %fusion.2 = bf16[32,36,128,4]{2,0,3,1:T(8,128)(2,1)S(1)} fusion(bf16[9,36,128,4]{2,0,3,1:T(8,128)(2,1)S(1)} %concatenate.33, f32[36]{0:T(128)S(1)} %and_convert_fusion.3, f32[32]{0:T(128)} %param.9, bf16[32,9,1,1]{0,1,2,3:T(8,128)(2,1)S(1)} %reshape.74), kind=kOutput, calls=%fused_computation.27 | convolution fusion | flops 12976128 | bytes 1512272 | tf_op jit(solution)/shard_map/ok,k...->o.../dot_general | solution.py:35
  32.4 0.4 fusion.6
  33.1 0.8 %fusion.7 = bf16[288,34,128,4]{2,0,3,1:T(8,128)(2,1)S(1)} fusion(bf16[288,34,128,4]{2,0,3,1:T(8,128)(2,1)S(1)} %slice_dynamic-update-slice_fusion.11, bf16[32,36,128,4]{2,0,3,1:T(8,128)(2,1)S(1)} %fusion.2), kind=kLoop, calls=%fused_computation.34 | loop fusion | bytes 2293760
  34.0 0.7 fusion.8
  35.0 0.7 fusion.9
  35.7 0.9 %fusion.10 = bf16[288,34,128,4]{2,0,3,1:T(8,128)(2,1)S(1)} fusion(bf16[288,34,128,4]{2,0,3,1:T(8,128)(2,1)S(1)} %fusion.9, bf16[32,36,128,4]{2,0,3,1:T(8,128)(2,1)S(1)} %fusion.2), kind=kLoop, calls=%fused_computation.37 | loop fusion | bytes 2293760
  36.8 0.7 fusion.11
  37.6 2.0 %fusion.3 = bf16[32,34,128,4]{2,0,3,1:T(8,128)(2,1)S(1)} fusion(bf16[288,34,128,4]{2,0,3,1:T(8,128)(2,1)S(1)} %fusion.11, f32[34]{0:T(128)S(1)} %and_convert_fusion.1, f32[32]{0:T(128)S(1)} %copy-done.2, bf16[32,288,1,1]{1,0,2,3:T(8,128)(2,1)S(1)} %reshape.75), kind=kOutput, calls=%fused_computation.28 | convolution fusion | flops 323092480 | bytes 11159816 | tf_op jit(solution)/shard_map/ok,k...->o.../dot_general | solution.py:35
  39.6 0.4 fusion.12
  40.1 0.8 %fusion.13 = bf16[288,32,128,4]{2,0,3,1:T(8,128)(2,1)S(1)} fusion(bf16[288,32,128,4]{2,0,3,1:T(8,128)(2,1)S(1)} %slice_dynamic-update-slice_fusion.14, bf16[32,34,128,4]{2,0,3,1:T(8,128)(2,1)S(1)} %fusion.3), kind=kLoop, calls=%fused_computation.43 | loop fusion | bytes 2162688
  40.9 0.7 fusion.14
  41.7 0.6 fusion.15
  42.4 0.8 %fusion.16 = bf16[288,32,128,4]{2,0,3,1:T(8,128)(2,1)S(1)} fusion(bf16[288,32,128,4]{2,0,3,1:T(8,128)(2,1)S(1)} %fusion.15, bf16[32,34,128,4]{2,0,3,1:T(8,128)(2,1)S(1)} %fusion.3), kind=kLoop, calls=%fused_computation.46 | loop fusion | bytes 2162688
  43.3 0.7 fusion.17
  44.1 5.1 %collective-permute-start.2 = (bf16[1,3,10,128]{3,0,2,1:T(2,128)(2,1)S(1)}, bf16[1,3,10,128]{3,0,2,1:T(2,128)(2,1)S(1)}, u32[]{:S(2)}, u32[]{:S(2)}) collective-permute-start(bf16[1,3,10,128]{3,0,2,1:T(2,128)(2,1)S(1)} %copy.33), channel_id=1, source_target_pairs={{0,1},{1,2},{2,3},{4,5},{5,6},{6,7},{8,9},{9,10},{10,11},{12,13},{... | collective-permute-start | bytes 23048 | tf_op jit(solution)/shard_map/ppermute | solution.py:14
  49.3 1.3 %fusion.4 = f32[3,4,32,128]{3,0,1,2:T(4,128)S(1)} fusion(bf16[288,32,128,4]{2,0,3,1:T(8,128)(2,1)S(1)} %fusion.17, f32[3]{0:T(128)S(1)} %copy-done.1, bf16[3,288,1,1]{1,0,2,3:T(4,128)(2,1)S(1)} %reshape.76), kind=kOutput, calls=%fused_computation.30 | convolution fusion | flops 28360704 | bytes 9635532 | tf_op jit(solution)/shard_map/ok,k...->o.../dot_general | solution.py:35
  50.6 2.1 %collective-permute-start.3 = (bf16[1,3,10,128]{3,0,2,1:T(2,128)(2,1)S(1)}, bf16[1,3,10,128]{3,0,2,1:T(2,128)(2,1)S(1)}, u32[]{:S(2)}, u32[]{:S(2)}) collective-permute-start(bf16[1,3,10,128]{3,0,2,1:T(2,128)(2,1)S(1)} %copy.34), channel_id=1, source_target_pairs={{1,0},{2,1},{3,2},{5,4},{6,5},{7,6},{9,8},{10,9},{11,10},{13,12},{... | collective-permute-start | bytes 23048 | tf_op jit(solution)/shard_map/ppermute | solution.py:15
  52.9 4.3 %collective-permute-done.3 = bf16[1,3,10,128]{3,0,2,1:T(2,128)(2,1)S(1)} collective-permute-done((bf16[1,3,10,128]{3,0,2,1:T(2,128)(2,1)S(1)}, bf16[1,3,10,128]{3,0,2,1:T(2,128)(2,1)S(1)}, u32[]{:S(2)}, u32[]{:S(2)}) %collective-permute-start.3) | collective-permute-done | bytes 7712 | tf_op jit(solution)/shard_map/ppermute | solution.py:15
  57.2 1.4 %fusion.26 = (bf16[1,36,8,128]{3,0,2,1:T(2,128)(2,1)S(1)}, bf16[1,36,8,128]{3,0,2,1:T(2,128)(2,1)S(1)}, bf16[1,36,8,128]{3,0,2,1:T(2,128)(2,1)S(1)}, bf16[1,36,8...) fusion(bf16[1,38,10,128]{3,0,2,1:T(2,128)(2,1)S(1)} %constant_d, ...), kind=kLoop, calls=%fused_computation.88 | loop fusion | bytes 1327104 | tf_op jit(solution)/shard_map/slice | solution.py:33
  58.6 5.5 %concatenate.29 = bf16[9,36,8,128]{3,0,2,1:T(8,128)(2,1)S(1)} concatenate(bf16[1,36,8,128]{3,0,2,1:T(2,128)(2,1)S(1)} %get-tuple-element.17, bf16[1,36,8,128]{3,0,2,1:T(2,128)(2,1)S(1)} %get-tuple-element.16, bf16[1,36,8,128]{3,0,2,1:T(2,128)(2,1)S(1)} %get-tuple-element.15, bf16[1,36,8,128]{3,0,2,1:T(2,128)(2,1)S(1)} %get-tuple-element.14, ...), dimensions={0} | concatenate | bytes 1327104 | tf_op jit(solution)/shard_map/concatenate | solution.py:34
  64.0 1.0 %fusion = bf16[32,36,8,128]{3,0,2,1:T(8,128)(2,1)S(1)} fusion(f32[8]{0:T(128)S(1)} %and_convert_fusion.2, f32[36]{0:T(128)S(1)} %and_convert_fusion.3, f32[32]{0:T(128)S(1)} %copy-done.3, bf16[9,36,8,128]{3,0,2,1:T(8,128)(2,1)S(1)} %concatenate.29, bf16[32,9,1,1]{0,1,2,3:T(8,128)(2,1)S(1)} %reshape.71), kind=kOutput, calls=%fused_computation.14 | convolution fusion | flops 27131904 | bytes 3023728 | tf_op jit(solution)/shard_map/ok,k...->o.../dot_general | solution.py:35
  65.1 0.4 slice_dynamic-update-slice_fusion.8
  65.5 0.5 slice_dynamic-update-slice_fusion.7
  66.0 0.5 slice_dynamic-update-slice_fusion.6
  66.5 0.5 slice_dynamic-update-slice_fusion.5
  66.9 0.5 slice_dynamic-update-slice_fusion.4
  67.5 0.5 slice_dynamic-update-slice_fusion.3
  67.9 0.5 slice_dynamic-update-slice_fusion.2
  68.4 0.5 slice_dynamic-update-slice_fusion.1
  68.9 0.5 slice_dynamic-update-slice_fusion
  69.4 2.9 %fusion.1 = bf16[32,34,6,128]{3,0,2,1:T(8,128)(2,1)S(1)} fusion(f32[6]{0:T(128)S(1)} %and_convert_fusion, f32[34]{0:T(128)S(1)} %and_convert_fusion.1, f32[32]{0:T(128)S(1)} %copy-done.2, bf16[288,34,6,128]{3,0,2,1:T(8,128)(2,1)S(1)} %slice_dynamic-update-slice_fusion, bf16[32,288,1,1]{1,0,2,3:T(8,128)(2,1)S(1)} %reshape.72), kind=kOutput, calls=%fused_computation.26 | convolution fusion | flops 485474304 | bytes 16730400 | tf_op jit(solution)/shard_map/ok,k...->o.../dot_general | solution.py:35
  73.7 1.3 %fusion.5 = f32[3,4,32,128]{3,0,1,2:T(4,128)S(1)} fusion(bf16[288,32,4,128]{3,0,2,1:T(8,128)(2,1)S(1)} %slice_dynamic-update-slice_fusion.15, f32[3]{0:T(128)S(1)} %copy-done.1, bf16[3,288,1,1]{1,0,2,3:T(4,128)(2,1)S(1)} %reshape.73), kind=kOutput, calls=%fused_computation.32 | convolution fusion | flops 28360704 | bytes 9635532 | tf_op jit(solution)/shard_map/ok,k...->o.../dot_general | solution.py:35
  75.6 0.8 %copy.24 = f32[4,4,32,128]{3,2,1,0:T(8,128)} copy(f32[4,4,32,128]{3,0,1,2:T(4,128)S(1)} %pad_maximum_fusion) | data formatting | bytes 524288 | tf_op jit(solution)/shard_map/stack | solution.py:85
  (50 shorter events, 3.9 us)
Async XLA Ops:
  0.8 43.2 %collective-permute-start.1 = (bf16[3,32,128]{2,1,0:T(8,128)(2,1)S(1)}, bf16[3,32,128]{2,1,0:T(8,128)(2,1)S(1)}, u32[]{:S(2)}, u32[]{:S(2)}) collective-permute-start(bf16[3,32,128]{2,1,0:T(8,128)(2,1)S(1)} %get-tuple-element.32), channel_id=1, source_target_pairs={{4,0},{8,4},{12,8},{16,12},{20,16},{24,20},{28,24},{32,28},{36,32}... | collective-permute-start | bytes 73736 | tf_op jit(solution)/shard_map/ppermute | solution.py:15
  13.2 30.8 %collective-permute-start = (bf16[3,32,128]{2,1,0:T(8,128)(2,1)S(1)}, bf16[3,32,128]{2,1,0:T(8,128)(2,1)S(1)}, u32[]{:S(2)}, u32[]{:S(2)}) collective-permute-start(bf16[3,32,128]{2,1,0:T(8,128)(2,1)S(1)} %get-tuple-element.31), channel_id=1, source_target_pairs={{0,4},{4,8},{8,12},{12,16},{16,20},{20,24},{24,28},{28,32},{32,36}... | collective-permute-start | bytes 73736 | tf_op jit(solution)/shard_map/ppermute | solution.py:14
  15.9 12.5 %collective-permute-start.4 = (bf16[1,3,128,4]{2,0,3,1:T(2,128)(2,1)S(1)}, bf16[1,3,128,4]{2,0,3,1:T(2,128)(2,1)S(1)}, u32[]{:S(2)}, u32[]{:S(2)}) collective-permute-start(bf16[1,3,128,4]{2,0,3,1:T(2,128)(2,1)S(1)} %copy.35), channel_id=1, source_target_pairs={{0,1},{1,2},{2,3},{4,5},{5,6},{6,7},{8,9},{9,10},{10,11},{12,13},{... | collective-permute-start | bytes 9224 | tf_op jit(solution)/shard_map/ppermute | solution.py:14
  21.3 7.9 %collective-permute-start.5 = (bf16[1,3,128,4]{2,0,3,1:T(2,128)(2,1)S(1)}, bf16[1,3,128,4]{2,0,3,1:T(2,128)(2,1)S(1)}, u32[]{:S(2)}, u32[]{:S(2)}) collective-permute-start(bf16[1,3,128,4]{2,0,3,1:T(2,128)(2,1)S(1)} %copy.36), channel_id=1, source_target_pairs={{1,0},{2,1},{3,2},{5,4},{6,5},{7,6},{9,8},{10,9},{11,10},{13,12},{... | collective-permute-start | bytes 9224 | tf_op jit(solution)/shard_map/ppermute | solution.py:15
  32.9 4.7 %copy-start.2 = (f32[32]{0:T(128)S(1)}, f32[32]{0:T(128)}, u32[]{:S(2)}) copy-start(f32[32]{0:T(128)} %param.11) | copy-start | bytes 388
  39.5 4.5 %copy-start = (bf16[4,32,128]{2,1,0:T(8,128)(2,1)S(1)}, bf16[4,32,128]{2,1,0:T(8,128)(2,1)}, u32[]{:S(2)}) copy-start(bf16[4,32,128]{2,1,0:T(8,128)(2,1)} %param.7) | copy-start | bytes 98308
  39.5 9.7 %copy-start.1 = (f32[3]{0:T(128)S(1)}, f32[3]{0:T(128)}, u32[]{:S(2)}) copy-start(f32[3]{0:T(128)} %param.13) | copy-start | bytes 40
  44.1 19.9 %copy-start.3 = (f32[32]{0:T(128)S(1)}, f32[32]{0:T(128)}, u32[]{:S(2)}) copy-start(f32[32]{0:T(128)} %param.9) | copy-start | bytes 388
  44.1 8.6 %collective-permute-start.2 = (bf16[1,3,10,128]{3,0,2,1:T(2,128)(2,1)S(1)}, bf16[1,3,10,128]{3,0,2,1:T(2,128)(2,1)S(1)}, u32[]{:S(2)}, u32[]{:S(2)}) collective-permute-start(bf16[1,3,10,128]{3,0,2,1:T(2,128)(2,1)S(1)} %copy.33), channel_id=1, source_target_pairs={{0,1},{1,2},{2,3},{4,5},{5,6},{6,7},{8,9},{9,10},{10,11},{12,13},{... | collective-permute-start | bytes 23048 | tf_op jit(solution)/shard_map/ppermute | solution.py:14
  50.6 6.6 %collective-permute-start.3 = (bf16[1,3,10,128]{3,0,2,1:T(2,128)(2,1)S(1)}, bf16[1,3,10,128]{3,0,2,1:T(2,128)(2,1)S(1)}, u32[]{:S(2)}, u32[]{:S(2)}) collective-permute-start(bf16[1,3,10,128]{3,0,2,1:T(2,128)(2,1)S(1)} %copy.34), channel_id=1, source_target_pairs={{1,0},{2,1},{3,2},{5,4},{6,5},{7,6},{9,8},{10,9},{11,10},{13,12},{... | collective-permute-start | bytes 23048 | tf_op jit(solution)/shard_map/ppermute | solution.py:15
where the time goes:
time: 77 us; the launch traced here: 76.4 us
  local copies, waits for them, and re-layouts  32.4 us (42%)
  starting transfers between devices  28.8 us (37%)
  matrix products  9.74 us (13%)
  waiting for transfers between devices  4.27 us (6%)
    ppermute x3, starting transfers between devices, with_halo(): after = lax.ppermute(initial, axis, down)  16.4 us
    unnamed x48, local copies, waits for them, and re-layouts  14 us
    ppermute x3, starting transfers between devices, with_halo(): before = lax.ppermute(last, axis, up)  12.4 us
    dot_general x6, matrix products, apply_layer(): jnp.einsum('ok,k...->o...', kernel, stacked, preferred_element_type=jnp.f...  9.74 us
    concatenate x6, local copies, waits for them, and re-layouts, apply_layer(): stacked = jnp.concatenate(taps, axis=0)  8.66 us
    ppermute x3, waiting for transfers between devices, with_halo(): after = lax.ppermute(initial, axis, down)  4.26 us
    another operation x3, local copies, waits for them, and re-layouts, flatten_kernel(): return kernel.transpose(2, 0, 1, 3).reshape(outputs, 9 * inputs)  2.33 us
    slice x2, local copies, waits for them, and re-layouts, apply_layer(): taps.append(lax.slice_in_dim(sliced, col_shift, col_shift + cols, axis=2))  2.18 us
  transfers between devices with their start and end apart: 6, of which 1 were waited for; matrix products, arithmetic and copies ran while one was open for 30% of the time, Pallas kernels for 0%

commit v1 on v0

v1 whole, which is shorter than its diff:
```python
import jax
import jax.numpy as jnp
from jax import lax
from jax.experimental import pallas as pl
from jax.experimental.pallas import tpu as pltpu
from jax.sharding import PartitionSpec as P

MESH = pl.DeviceIdType.MESH
F32 = jnp.float32
BF16 = jnp.bfloat16

SIDES = [(ds, dr) for ds in (-1, 0, 1) for dr in (-1, 0, 1) if ds or dr]
RUN = 32


def iota(shape, dim):
    return lax.broadcasted_iota(jnp.int32, shape, dim)


def spread(rows, lanes):
    return ((iota((rows, lanes), 1) & 31) == iota((rows, lanes), 0)).astype(BF16)


def dot(a, b):
    return jnp.dot(a, b, preferred_element_type=F32)


def span(step, own, low, high):
    return {0: own, 1: low, -1: high}[step]


def exchange_kernel(
    img, k1, b1, k2, b2, k3, b3,
    ext, w1z, w2z, w3z, b2c, brow, xyp,
    k1v, b1v, k2v, b2v, k3v, b3v, w1x, w2x, w3x, imx, h1c, h1l, h1r, h2x,
    load_sem, send_sem, recv_sem,
):
    s = lax.axis_index("slab")
    r = lax.axis_index("row")
    slabs = lax.axis_size("slab")
    rows = lax.axis_size("row")
    place = lax.rem(s, RUN)

    def inside(ds, dr):
        return (s + ds >= 0) & (s + ds < slabs) & (r + dr >= 0) & (r + dr < rows)

    def later(ds, dr):
        if ds == 0:
            return jnp.bool_(dr > 0)
        if ds > 0:
            return place != RUN - 1
        return place == 0

    barrier = pltpu.get_barrier_semaphore()
    greeted = jnp.int32(0)
    for ds, dr in SIDES:
        here = inside(ds, dr)
        after = later(ds, dr)
        greeted += (here & ~after).astype(jnp.int32)

        @pl.when(here & after)
        def _():
            pl.semaphore_signal(barrier, inc=1, device_id=(s + ds, r + dr), device_id_type=MESH)

    copies = []
    for n, (ds, dr) in enumerate(SIDES):
        zs, zd = span(ds, ((0, 4), (3, 7)), ((1, 4), (0, 3)), ((0, 3), (7, 10)))
        ys, yd = span(dr, ((0, 32), (16, 48)), ((16, 32), (0, 16)), ((0, 16), (48, 64)))
        copies.append(
            pltpu.make_async_remote_copy(
                src_ref=img.at[zs[0] : zs[1], ys[0] : ys[1]],
                dst_ref=ext.at[zd[0] : zd[1], yd[0] : yd[1]],
                send_sem=send_sem.at[n],
                recv_sem=recv_sem.at[n],
                device_id=(s + ds, r + dr),
                device_id_type=MESH,
            )
        )

    @pl.when(greeted > 0)
    def _():
        pl.semaphore_wait(barrier, greeted)

    for n, (ds, dr) in enumerate(SIDES):

        @pl.when(inside(ds, dr) & ~later(ds, dr))
        def _():
            copies[n].start()

    loads = [
        pltpu.make_async_copy(a, b, load_sem.at[n])
        for n, (a, b) in enumerate(
            [(img, ext.at[3:7, 16:48]), (k1, k1v), (b1, b1v), (k2, k2v), (b2, b2v), (k3, k3v), (b3, b3v)]
        )
    ]
    for load in loads:
        load.start()

    for ds, dr in SIDES:
        z0, z1 = {-1: (0, 3), 0: (3, 7), 1: (7, 10)}[ds]
        y0, y1 = {-1: (0, 16), 0: (16, 48), 1: (48, 64)}[dr]

        @pl.when(~inside(ds, dr))
        def _():
            ext[z0:z1, y0:y1, :] = jnp.zeros((z1 - z0, y1 - y0, 128), BF16)

    for load in loads:
        load.wait()

    bias = b1v[...]
    high = bias.astype(BF16).astype(F32)
    mid = (bias - high).astype(BF16).astype(F32)
    low = bias - high - mid
    pieces = [k1v[a].astype(F32)[b : b + 1] for a in range(3) for b in range(3)] + [high, mid, low]
    row = iota((16, 32), 0)
    kk = jnp.zeros((16, 32), F32)
    for n, piece in enumerate(pieces):
        kk = jnp.where(row == n, jnp.broadcast_to(piece, (16, 32)), kk)
    kt = dot(kk.astype(BF16), spread(32, 512))

    def taps(height, lanes, b, first):
        out = jnp.zeros((height, lanes), F32)
        gap = iota((height, lanes), 0) - (iota((height, lanes), 1) >> 5) - first
        for a in range(3):
            n = 3 * a + b
            out = jnp.where(gap == a, jnp.broadcast_to(kt[n : n + 1, :lanes], (height, lanes)), out)
        return out

    def biases(out, first):
        height, lanes = out.shape
        at = iota((height, lanes), 0) - first
        for m in range(3):
            out = jnp.where(at == m, jnp.broadcast_to(kt[9 + m : 10 + m, :lanes], (height, lanes)), out)
        return out

    tall = jnp.concatenate(
        [taps(32, 512, b, 13) for b in range(3)] + [biases(jnp.zeros((32, 512), F32), 0)], axis=0
    )
    w1x[...] = tall.T.astype(BF16)
    flat = jnp.concatenate(
        [taps(16, 256, 0, 0), biases(taps(16, 256, 1, 0), 10), taps(16, 256, 2, 0), jnp.zeros((80, 256), F32)], axis=0
    )
    w1z[...] = flat.T[:, :48].astype(BF16)

    z_of = s * 4 + (iota((32, 256), 1) >> 5)
    in_two = (z_of >= 2) & (z_of < 4 * slabs + 2)
    part = iota((32, 256), 1) >> 5
    wide = dot(k2v[...].reshape(288, 32), spread(32, 256))
    for b in range(3):
        for o in range(6):
            block = jnp.zeros((32, 256), F32)
            for a in range(3):
                n = (3 * a + b) * 32
                block = jnp.where(part == o + a, wide[n : n + 32], block)
            w2x[o * 32 : o * 32 + 32, b * 256 : b * 256 + 256] = block.astype(BF16)
            w2z[o * 32 : o * 32 + 32, b * 256 : b * 256 + 256] = jnp.where(in_two, block, 0.0).astype(BF16)
    column = jnp.sum(
        jnp.where(iota((32, 32), 0) == iota((32, 32), 1), jnp.broadcast_to(b2v[...], (32, 32)), 0.0), axis=1, keepdims=True
    )
    for o in range(6):
        b2c[o * 32 : o * 32 + 32, :] = jnp.broadcast_to(column, (32, 128))

    group = iota((48, 32), 0) >> 2
    lasts = []
    for a in range(3):
        last = jnp.zeros((48, 32), F32)
        for b in range(3):
            line = k3v[a, b].astype(F32)
            for f in range(3):
                last = jnp.where(group == 4 * b + f, jnp.broadcast_to(line[f : f + 1], (48, 32)), last)
        lasts.append(last)
    wide3 = dot(jnp.concatenate(lasts, axis=0).astype(BF16), spread(32, 192))
    part3 = (iota((48, 192), 1) >> 5) - (iota((48, 192), 0) & 3)
    last = jnp.zeros((48, 192), F32)
    for a in range(3):
        last = jnp.where(part3 == a, wide3[48 * a : 48 * a + 48], last)
    z_of = s * 4 + (iota((48, 192), 1) >> 5)
    w3x[...] = last.astype(BF16)
    w3z[...] = jnp.where((z_of >= 1) & (z_of < 4 * slabs + 1), last, 0.0).astype(BF16)

    kind = iota((16, 128), 0) >> 2
    flow = [jnp.broadcast_to(b3v[0:1, f : f + 1], (16, 128)) for f in range(3)]
    brow[...] = jnp.where(kind == 0, flow[0], 0.0)
    bias_xy = jnp.where(kind == 0, 0.5 * (flow[0] + flow[1]), jnp.where(kind == 1, flow[1], flow[2]))
    scale_xy = jnp.where(kind == 1, 1.0, 0.5)

    def answer(ds, dr, extra=True):
        @pl.when(inside(ds, dr) & later(ds, dr) & extra)
        def _():
            copies[SIDES.index((-ds, -dr))].wait_recv()
            copies[SIDES.index((ds, dr))].start()

    def collect(ds, dr):
        @pl.when(inside(ds, dr) & ~later(ds, dr))
        def _():
            copies[SIDES.index((-ds, -dr))].wait_recv()

    answer(0, 1)
    for dr in (0, -1, 1):
        answer(1, dr)
    collect(0, -1)

    lane = iota((64, 128), 1)
    for z in range(4):
        plane = ext[3 + z].astype(F32)
        at = pl.ds(z * 128, 128)
        imx[0, :, at] = jnp.where(lane == 0, 0.0, pltpu.roll(plane, 1, 1)).astype(BF16)
        imx[1, :, at] = plane.astype(BF16)
        imx[2, :, at] = jnp.where(lane == 127, 0.0, pltpu.roll(plane, 127, 1)).astype(BF16)

    def shifted(values, by):
        edge = iota((values.shape[0], 128), 1) == (0 if by > 0 else 127)
        halves = [jnp.where(edge, 0.0, pltpu.roll(values[:, h : h + 128], by % 128, 1)) for h in (0, 128)]
        return jnp.concatenate(halves, axis=1)

    bias_two = jnp.concatenate([b2c[...]] * 2, axis=1)

    def pair(t, carry):
        cols = pl.ds(pl.multiple_of(t * 256, 256), 256)
        for j, height in ((0, 512), (1, 512), (2, 128)):
            window = [imx[b, 16 * j : 16 * j + 32, cols] for b in range(3)]
            rhs = jnp.concatenate(window + [jnp.ones((32, 256), BF16)], axis=0)
            hidden = jnp.maximum(dot(w1x[:height], rhs), 0.0)
            h1c[512 * j : 512 * j + height] = hidden.astype(BF16)
            h1l[512 * j : 512 * j + height] = shifted(hidden, 1).astype(BF16)
            h1r[512 * j : 512 * j + height] = shifted(hidden, -1).astype(BF16)

        for ref in (h1c, h1l, h1r):

            @pl.when(r == 0)
            def _():
                ref[:64] = jnp.zeros((64, 256), BF16)

            @pl.when(r == rows - 1)
            def _():
                ref[1088:] = jnp.zeros((64, 256), BF16)

        for first in (0, 6, 12, 18, 24, 28):
            at = first * 32
            rhs = jnp.concatenate([ref[at : at + 256] for ref in (h1l, h1c, h1r)], axis=0)
            h2x[at : at + 192] = jnp.maximum(dot(w2x[...], rhs) + bias_two, 0.0).astype(BF16)

        @pl.when(r == 0)
        def _():
            h2x[:32] = jnp.zeros((32, 256), BF16)

        @pl.when(r == rows - 1)
        def _():
            h2x[1056:] = jnp.zeros((32, 256), BF16)

        for k in range(8):
            terms = dot(w3x[...], h2x[128 * k : 128 * k + 192])
            total = shifted(terms[:16], 1) + terms[16:32] + shifted(terms[32:], -1)
            for h in range(2):
                flows = total[:, 128 * h : 128 * h + 128] * scale_xy + bias_xy
                for f in range(3):
                    xyp[pl.ds((4 * f + 2 * t + h) * 32 + 4 * k, 4), :] = flows[4 * f : 4 * f + 4]
        return carry

    lax.fori_loop(0, 2, pair, 0)

    for dr in (0, -1, 1):
        answer(-1, dr)
    for dr in (0, -1, 1):
        collect(1, dr)
        collect(-1, dr)
    for n, (ds, dr) in enumerate(SIDES):

        @pl.when(inside(ds, dr))
        def _():
            copies[n].wait_send()


def yz_kernel(ext, w1, w2, w3, b2c, brow, xyp, out, imt, h1, h2, p3):
    r = lax.axis_index("row")
    first = jnp.where(r == 0, 0.0, 1.0)
    final = jnp.where(r == lax.axis_size("row") - 1, 0.0, 1.0)

    for z in range(10):
        imt[pl.ds(z, 64, stride=16), :] = ext[z].astype(F32)
    for z in range(10, 16):
        imt[pl.ds(z, 64, stride=16), :] = jnp.ones((64, 128), F32)

    bias_two = jnp.concatenate([b2c[...]] * 2, axis=1)
    kind = iota((16, 128), 0) >> 2
    scale = jnp.where(kind == 0, 1.0, 0.5)
    add = brow[...]

    def one(j):
        rhs = jnp.concatenate([imt[(j + h + 13) * 16 : (j + h + 16) * 16, :].astype(BF16) for h in range(2)], axis=1)
        hidden = jnp.maximum(dot(w1[...], rhs), 0.0)
        if j == 0:
            hidden = hidden * first
        if j == 34:
            hidden = hidden * final
        h1[:, j * 128 : j * 128 + 256] = hidden.astype(BF16)

    def two(j):
        rhs = jnp.concatenate([h1[:, (j + b) * 128 : (j + b) * 128 + 256] for b in range(3)], axis=0)
        hidden = jnp.maximum(dot(w2[...], rhs) + bias_two, 0.0)
        if j == 0:
            hidden = jnp.concatenate([hidden[:, :128] * first, hidden[:, 128:]], axis=1)
        if j == 32:
            hidden = jnp.concatenate([hidden[:, :128], hidden[:, 128:] * final], axis=1)
        h2[:, j * 128 : j * 128 + 256] = hidden.astype(BF16)

    def three(j):
        p3[:, j * 128 : j * 128 + 256] = dot(w3[...], h2[:, j * 128 : j * 128 + 256])

    def finish(y):
        total = sum(p3[16 * b : 16 * b + 16, (y + b) * 128 : (y + b) * 128 + 128] for b in range(3))
        flows = total * scale + add
        out[pl.ds(y, 8, stride=32), :] = flows[:8]
        out[pl.ds(384 + y, 4, stride=32), :] = flows[8:12]

    for step in range(22):
        if step < 18:
            one(2 * step)
        if 2 <= step < 19:
            two(2 * (step - 2))
        if 3 <= step < 20:
            three(2 * (step - 3))
        if 5 <= step < 21:
            finish(2 * (step - 5))
            finish(2 * (step - 5) + 1)
    out[128:256, :] = out[128:256, :] + xyp[:128]
    out[256:384, :] = xyp[128:256]
    out[384:512, :] = out[384:512, :] + xyp[256:]


def local(image, first_kernel, first_bias, middle_kernel, middle_bias, last_kernel, last_bias):
    args = (
        image,
        first_kernel.reshape(3, 3, 32),
        first_bias.reshape(1, 32),
        middle_kernel,
        middle_bias.reshape(1, 32),
        last_kernel,
        last_bias.reshape(1, 3),
    )
    args = [pltpu.with_memory_space_constraint(a, pltpu.HBM) for a in args]
    shape = jax.ShapeDtypeStruct
    vmem = pl.BlockSpec(memory_space=pltpu.VMEM)
    outs = [
        shape((10, 64, 128), BF16),
        shape((256, 48), BF16),
        shape((192, 768), BF16),
        shape((48, 192), BF16),
        shape((192, 128), F32),
        shape((16, 128), F32),
        shape((384, 128), F32),
    ]
    made = pl.pallas_call(
        exchange_kernel,
        out_shape=outs,
        in_specs=[pl.BlockSpec(memory_space=pltpu.HBM)] * 7,
        out_specs=[vmem] * 7,
        scratch_shapes=[
            pltpu.VMEM((3, 3, 32), BF16),
            pltpu.VMEM((1, 32), F32),
            pltpu.VMEM((3, 3, 32, 32), BF16),
            pltpu.VMEM((1, 32), F32),
            pltpu.VMEM((3, 3, 3, 32), BF16),
            pltpu.VMEM((1, 3), F32),
            pltpu.VMEM((512, 128), BF16),
            pltpu.VMEM((192, 768), BF16),
            pltpu.VMEM((48, 192), BF16),
            pltpu.VMEM((3, 64, 512), BF16),
            pltpu.VMEM((1152, 256), BF16),
            pltpu.VMEM((1152, 256), BF16),
            pltpu.VMEM((1152, 256), BF16),
            pltpu.VMEM((1088, 256), BF16),
            pltpu.SemaphoreType.DMA((7,)),
            pltpu.SemaphoreType.DMA((8,)),
            pltpu.SemaphoreType.DMA((8,)),
        ],
        compiler_params=pltpu.CompilerParams(collective_id=0, has_side_effects=True, vmem_limit_bytes=24 * 2**20),
    )(*args)
    flows = pl.pallas_call(
        yz_kernel,
        out_shape=shape((512, 128), F32),
        in_specs=[vmem] * 7,
        out_specs=vmem,
        scratch_shapes=[
            pltpu.VMEM((1024, 128), F32),
            pltpu.VMEM((256, 36 * 128), BF16),
            pltpu.VMEM((192, 34 * 128), BF16),
            pltpu.VMEM((48, 34 * 128), F32),
        ],
        compiler_params=pltpu.CompilerParams(vmem_limit_bytes=24 * 2**20),
    )(*made)
    return flows.reshape(4, 4, 32, 128)


def solution(mesh):
    placed = (P("slab", "row", None), P(), P(), P(), P(), P(), P())
    return jax.shard_map(
        local, mesh=mesh, in_specs=placed, out_specs=P(None, "slab", "row", None), check_vma=False
    )
```

time: 77 us -> 21.5 us (0.28)
  local copies, waits for them, and re-layouts: 32.4 us -> 0 us
  starting transfers between devices: 28.8 us -> 0 us
  Pallas kernels: 0 us -> 21.4 us
  matrix products: 9.74 us -> 0 us
  waiting for transfers between devices: 4.27 us -> 0 us
    ppermute x6 -> x0, starting transfers between devices: 28.8 us -> none  [the longest x3 16.4 us: with_halo(): after = lax.ppermute(initial, axis, down)]
    pallas_call x0 -> x2, Pallas kernels: none -> 21.4 us  [the longest x1 17 us: local(): pl.pallas_call(exchange_kernel, out_shape=outs, in_specs=[pl.BlockSpec(me...]
    unnamed x48 -> x0, local copies, waits for them, and re-layouts: 14 us -> none
    dot_general x6 -> x0, matrix products: 9.74 us -> none  [apply_layer(): jnp.einsum('ok,k...->o...', kernel, stacked, preferred_element_type=jnp.f...]
    concatenate x8 -> x0, local copies, waits for them, and re-layouts: 8.7 us -> none  [the longest x6 8.66 us: apply_layer(): stacked = jnp.concatenate(taps, axis=0)]
    ppermute x6 -> x0, waiting for transfers between devices: 4.27 us -> none  [the longest x3 4.26 us: with_halo(): after = lax.ppermute(initial, axis, down)]
    slice x5 -> x0, local copies, waits for them, and re-layouts: 3.74 us -> none  [the longest x2 2.18 us: apply_layer(): taps.append(lax.slice_in_dim(sliced, col_shift, col_shift + cols, axis=2))]
    another operation x4 -> x0, local copies, waits for them, and re-layouts: 3.11 us -> none  [the longest x3 2.33 us: flatten_kernel(): return kernel.transpose(2, 0, 1, 3).reshape(outputs, 9 * inputs)]
  transfers between devices with their start and end apart: 6 -> 0, of which waited for: 1 -> 0; matrix products, arithmetic and copies ran while one was open for 30% -> 0% of each run, Pallas kernels for 0% -> 0%
where the time goes in v1:
time: 21.5 us; the launch traced here: 21.4 us
  Pallas kernels  21.4 us (100%)
    pallas_call x1, Pallas kernels, local(): pl.pallas_call(exchange_kernel, out_shape=outs, in_specs=[pl.BlockSpec(me...  17 us
    pallas_call x1, Pallas kernels, local(): pl.pallas_call(yz_kernel, out_shape=shape((512, 128), F32), in_specs=[vme...  4.41 us

profile of v1, /device:TPU:7, one launch (start us, length us, event | category | flops | bytes accessed | tf_op | source)
XLA Modules:
  0.0 21.4 jit_solution(10939022813842652044)
XLA Ops:
  0.0 17.0 %shard_map.73 = (bf16[10,64,128]{2,1,0:T(8,128)(2,1)S(1)}, bf16[256,48]{1,0:T(8,128)(2,1)S(1)}, bf16[192,768]{1,0:T(8,128)(2,1)S(1)}, bf16[48,192]{1,0:T(8,128)(...) custom-call(bf16[4,32,128]{2,1,0:T(8,128)(2,1)} %img.1, ...), custom_call_target="tpu_custom_call" | custom-call | tf_op jit(solution)/shard_map/pallas_call | solution.py:353
  17.0 4.4 %shard_map.74 = f32[512,128]{1,0:T(8,128)} custom-call(bf16[10,64,128]{2,1,0:T(8,128)(2,1)S(1)} %get-tuple-element.12.ext, bf16[256,48]{1,0:T(8,128)(2,1)S(1)} %get-tuple-element.13.w1, bf16[192,768]{1,0:T(8,128)(2,1)S(1)} %get-tuple-element.14.w2, bf16[48,192]{1,0:T(8,128)(2,1)S(1)} %get-tuple-element.15.w3, f32[192,128]{1,0:T(8,128)S(1)} %get-tuple-element.16.b2c, ...), custom_call_target="tpu_custom_call" | custom-call | tf_op jit(solution)/shard_map/pallas_call | solution.py:379

commit v2 on v1

--- a/solution.py
+++ b/solution.py
@@ -9,7 +9,7 @@
 F32 = jnp.float32
 BF16 = jnp.bfloat16
 
-SIDES = [(ds, dr) for ds in (-1, 0, 1) for dr in (-1, 0, 1) if ds or dr]
+SIDES = [(ds, dr) for ds in (1, -1, 0) for dr in (0, 1, -1) if ds or dr]
 RUN = 32
 
 
@@ -29,9 +29,10 @@
     return {0: own, 1: low, -1: high}[step]
 
 
-def exchange_kernel(
+def kernel(
     img, k1, b1, k2, b2, k3, b3,
-    ext, w1z, w2z, w3z, b2c, brow, xyp,
+    out,
+    ext, w1z, w2z, w3z, b2c, xyp, imt, g1, g2, p3,
     k1v, b1v, k2v, b2v, k3v, b3v, w1x, w2x, w3x, imx, h1c, h1l, h1r, h2x,
     load_sem, send_sem, recv_sem,
 ):
@@ -40,52 +41,92 @@
     slabs = lax.axis_size("slab")
     rows = lax.axis_size("row")
     place = lax.rem(s, RUN)
+    wrap = place == RUN - 1
 
     def inside(ds, dr):
         return (s + ds >= 0) & (s + ds < slabs) & (r + dr >= 0) & (r + dr < rows)
 
-    def later(ds, dr):
+    def uneven(ds):
+        return wrap if ds == 0 else (wrap | (place == RUN - 2) if ds > 0 else wrap | (place == 0))
+
+    def first(ds, dr):
         if ds == 0:
-            return jnp.bool_(dr > 0)
+            return (r ^ 1) < ((r + dr) ^ 1)
         if ds > 0:
-            return place != RUN - 1
-        return place == 0
+            return jnp.bool_(False)
+        return jnp.bool_(True)
 
     barrier = pltpu.get_barrier_semaphore()
     greeted = jnp.int32(0)
     for ds, dr in SIDES:
-        here = inside(ds, dr)
-        after = later(ds, dr)
-        greeted += (here & ~after).astype(jnp.int32)
-
-        @pl.when(here & after)
+        greeted += (inside(ds, dr) & ~(uneven(ds) & first(ds, dr))).astype(jnp.int32)
+
+    def greet(ds, dr):
+        @pl.when(inside(ds, dr) & ~(uneven(ds) & ~first(ds, dr)))
         def _():
             pl.semaphore_signal(barrier, inc=1, device_id=(s + ds, r + dr), device_id_type=MESH)
 
-    copies = []
+    copies = {}
     for n, (ds, dr) in enumerate(SIDES):
         zs, zd = span(ds, ((0, 4), (3, 7)), ((1, 4), (0, 3)), ((0, 3), (7, 10)))
         ys, yd = span(dr, ((0, 32), (16, 48)), ((16, 32), (0, 16)), ((0, 16), (48, 64)))
-        copies.append(
-            pltpu.make_async_remote_copy(
-                src_ref=img.at[zs[0] : zs[1], ys[0] : ys[1]],
-                dst_ref=ext.at[zd[0] : zd[1], yd[0] : yd[1]],
-                send_sem=send_sem.at[n],
-                recv_sem=recv_sem.at[n],
-                device_id=(s + ds, r + dr),
-                device_id_type=MESH,
-            )
+        copies[ds, dr] = pltpu.make_async_remote_copy(
+            src_ref=img.at[zs[0] : zs[1], ys[0] : ys[1]],
+            dst_ref=ext.at[zd[0] : zd[1], yd[0] : yd[1]],
+            send_sem=send_sem.at[n],
+            recv_sem=recv_sem.at[n],
+            device_id=(s + ds, r + dr),
+            device_id_type=MESH,
         )
 
-    @pl.when(greeted > 0)
+    broad = pltpu.make_async_remote_copy(
+        src_ref=ext.at[3:6],
+        dst_ref=ext.at[7:10],
+        send_sem=send_sem.at[8],
+        recv_sem=recv_sem.at[8],
+        device_id=(s - 1, r),
+        device_id_type=MESH,
+    )
+    head = (place == 0) & (s > 0)
+    tail = wrap & (s < slabs - 1)
+
+    def meet_and_send():
+        @pl.when(greeted > 0)
+        def _():
+            pl.semaphore_wait(barrier, greeted)
+
+        for ds, dr in SIDES:
+
+            @pl.when(inside(ds, dr) & ~(uneven(ds) & first(ds, dr)))
+            def _():
+                copies[ds, dr].start()
+
+    def arrive(ds, dr):
+        @pl.when(inside(ds, dr))
+        def _():
+            copies[-ds, -dr].wait_recv()
+
+        @pl.when(inside(ds, dr) & uneven(ds) & first(ds, dr))
+        def _():
+            copies[ds, dr].start()
+
+    def arrive_head(dr):
+        @pl.when(head & inside(-1, dr))
+        def _():
+            copies[1, -dr].wait_recv()
+            if dr == 0:
+                broad.start()
+
+    greet(0, 1)
+    greet(0, -1)
+
+    @pl.when(wrap)
     def _():
-        pl.semaphore_wait(barrier, greeted)
-
-    for n, (ds, dr) in enumerate(SIDES):
-
-        @pl.when(inside(ds, dr) & ~later(ds, dr))
-        def _():
-            copies[n].start()
+        meet_and_send()
+
+    for ds in (1, -1):
+        for dr in (0, 1, -1):
+            greet(ds, dr)
 
     loads = [
         pltpu.make_async_copy(a, b, load_sem.at[n])
@@ -100,10 +141,12 @@
         z0, z1 = {-1: (0, 3), 0: (3, 7), 1: (7, 10)}[ds]
         y0, y1 = {-1: (0, 16), 0: (16, 48), 1: (48, 64)}[dr]
 
-        @pl.when(~inside(ds, dr))
+        @pl.when(~inside(ds, dr) & ~(tail if ds == 1 else jnp.bool_(False)))
         def _():
             ext[z0:z1, y0:y1, :] = jnp.zeros((z1 - z0, y1 - y0, 128), BF16)
 
+    for z in range(10, 16):
+        imt[pl.ds(z, 64, stride=16), :] = jnp.ones((64, 128), F32)
     for load in loads:
         load.wait()
 
@@ -180,25 +223,22 @@
 
     kind = iota((16, 128), 0) >> 2
     flow = [jnp.broadcast_to(b3v[0:1, f : f + 1], (16, 128)) for f in range(3)]
-    brow[...] = jnp.where(kind == 0, flow[0], 0.0)
+    bias_yz = jnp.where(kind == 0, flow[0], 0.0)
+    scale_yz = jnp.where(kind == 0, 1.0, 0.5)
     bias_xy = jnp.where(kind == 0, 0.5 * (flow[0] + flow[1]), jnp.where(kind == 1, flow[1], flow[2]))
     scale_xy = jnp.where(kind == 1, 1.0, 0.5)
 
-    def answer(ds, dr, extra=True):
-        @pl.when(inside(ds, dr) & later(ds, dr) & extra)
-        def _():
-            copies[SIDES.index((-ds, -dr))].wait_recv()
-            copies[SIDES.index((ds, dr))].start()
-
-    def collect(ds, dr):
-        @pl.when(inside(ds, dr) & ~later(ds, dr))
-        def _():
-            copies[SIDES.index((-ds, -dr))].wait_recv()
-
-    answer(0, 1)
-    for dr in (0, -1, 1):
-        answer(1, dr)
-    collect(0, -1)
+    @pl.when(~wrap)
+    def _():
+        meet_and_send()
+
+    arrive(0, 1)
+    arrive(0, -1)
+
+    @pl.when(wrap)
+    def _():
+        for dr in (0, 1, -1):
+            arrive(-1, dr)
 
     lane = iota((64, 128), 1)
     for z in range(4):
@@ -259,73 +299,99 @@
 
     lax.fori_loop(0, 2, pair, 0)
 
-    for dr in (0, -1, 1):
-        answer(-1, dr)
-    for dr in (0, -1, 1):
-        collect(1, dr)
-        collect(-1, dr)
-    for n, (ds, dr) in enumerate(SIDES):
-
-        @pl.when(inside(ds, dr))
-        def _():
-            copies[n].wait_send()
-
-
-def yz_kernel(ext, w1, w2, w3, b2c, brow, xyp, out, imt, h1, h2, p3):
-    r = lax.axis_index("row")
-    first = jnp.where(r == 0, 0.0, 1.0)
-    final = jnp.where(r == lax.axis_size("row") - 1, 0.0, 1.0)
-
-    for z in range(10):
-        imt[pl.ds(z, 64, stride=16), :] = ext[z].astype(F32)
-    for z in range(10, 16):
-        imt[pl.ds(z, 64, stride=16), :] = jnp.ones((64, 128), F32)
-
-    bias_two = jnp.concatenate([b2c[...]] * 2, axis=1)
-    kind = iota((16, 128), 0) >> 2
-    scale = jnp.where(kind == 0, 1.0, 0.5)
-    add = brow[...]
+    def turn(z0, z1, y0, y1):
+        for z in range(z0, z1):
+            imt[pl.ds(16 * y0 + z, y1 - y0, stride=16), :] = ext[z, y0:y1, :].astype(F32)
+
+    def arrive_high(dr):
+        @pl.when(~wrap)
+        def _():
+            arrive(1, dr)
+
+    def arrive_low(dr):
+        @pl.when(~wrap & ~head)
+        def _():
+            arrive(-1, dr)
+
+    turn(3, 7, 0, 64)
+    arrive_high(0)
+    arrive_high(-1)
+
+    @pl.when(tail)
+    def _():
+        broad.wait_recv()
+
+    turn(7, 10, 0, 48)
+    arrive_low(0)
+    arrive_low(-1)
+    arrive_head(0)
+    arrive_head(-1)
+    turn(0, 3, 0, 48)
+
+    top = jnp.where(r == 0, 0.0, 1.0)
+    bottom = jnp.where(r == rows - 1, 0.0, 1.0)
 
     def one(j):
         rhs = jnp.concatenate([imt[(j + h + 13) * 16 : (j + h + 16) * 16, :].astype(BF16) for h in range(2)], axis=1)
-        hidden = jnp.maximum(dot(w1[...], rhs), 0.0)
+        hidden = jnp.maximum(dot(w1z[...], rhs), 0.0)
         if j == 0:
-            hidden = hidden * first
+            hidden = hidden * top
         if j == 34:
-            hidden = hidden * final
-        h1[:, j * 128 : j * 128 + 256] = hidden.astype(BF16)
+            hidden = hidden * bottom
+        g1[:, j * 128 : j * 128 + 256] = hidden.astype(BF16)
 
     def two(j):
-        rhs = jnp.concatenate([h1[:, (j + b) * 128 : (j + b) * 128 + 256] for b in range(3)], axis=0)
-        hidden = jnp.maximum(dot(w2[...], rhs) + bias_two, 0.0)
+        rhs = jnp.concatenate([g1[:, (j + b) * 128 : (j + b) * 128 + 256] for b in range(3)], axis=0)
+        hidden = jnp.maximum(dot(w2z[...], rhs) + bias_two, 0.0)
         if j == 0:
-            hidden = jnp.concatenate([hidden[:, :128] * first, hidden[:, 128:]], axis=1)
+            hidden = jnp.concatenate([hidden[:, :128] * top, hidden[:, 128:]], axis=1)
         if j == 32:
-            hidden = jnp.concatenate([hidden[:, :128], hidden[:, 128:] * final], axis=1)
-        h2[:, j * 128 : j * 128 + 256] = hidden.astype(BF16)
+            hidden = jnp.concatenate([hidden[:, :128], hidden[:, 128:] * bottom], axis=1)
+        g2[:, j * 128 : j * 128 + 256] = hidden.astype(BF16)
 
     def three(j):
-        p3[:, j * 128 : j * 128 + 256] = dot(w3[...], h2[:, j * 128 : j * 128 + 256])
+        p3[:, j * 128 : j * 128 + 256] = dot(w3z[...], g2[:, j * 128 : j * 128 + 256])
 
     def finish(y):
         total = sum(p3[16 * b : 16 * b + 16, (y + b) * 128 : (y + b) * 128 + 128] for b in range(3))
-        flows = total * scale + add
+        flows = total * scale_yz + bias_yz
         out[pl.ds(y, 8, stride=32), :] = flows[:8]
         out[pl.ds(384 + y, 4, stride=32), :] = flows[8:12]
 
-    for step in range(22):
-        if step < 18:
-            one(2 * step)
-        if 2 <= step < 19:
-            two(2 * (step - 2))
-        if 3 <= step < 20:
-            three(2 * (step - 3))
-        if 5 <= step < 21:
-            finish(2 * (step - 5))
-            finish(2 * (step - 5) + 1)
+    for k in range(16):
+        one(2 * k)
+    for k in range(15):
+        two(2 * k)
+    for k in range(15):
+        three(2 * k)
+    for y in range(28):
+        finish(y)
+    arrive_high(1)
+    turn(7, 10, 48, 64)
+    arrive_low(1)
+    arrive_head(1)
+    turn(0, 3, 48, 64)
+    for k in range(16, 18):
+        one(2 * k)
+    for k in range(15, 17):
+        two(2 * k)
+    for k in range(15, 17):
+        three(2 * k)
+    for y in range(28, 32):
+        finish(y)
     out[128:256, :] = out[128:256, :] + xyp[:128]
     out[256:384, :] = xyp[128:256]
     out[384:512, :] = out[384:512, :] + xyp[256:]
+
+    for ds, dr in SIDES:
+
+        @pl.when(inside(ds, dr) & ~(head if ds == -1 else jnp.bool_(False)))
+        def _():
+            copies[ds, dr].wait_send()
+
+    @pl.when(head)
+    def _():
+        broad.wait_send()
 
 
 def local(image, first_kernel, first_bias, middle_kernel, middle_bias, last_kernel, last_bias):
@@ -341,21 +407,22 @@
     args = [pltpu.with_memory_space_constraint(a, pltpu.HBM) for a in args]
     shape = jax.ShapeDtypeStruct
     vmem = pl.BlockSpec(memory_space=pltpu.VMEM)
-    outs = [
-        shape((10, 64, 128), BF16),
-        shape((256, 48), BF16),
-        shape((192, 768), BF16),
-        shape((48, 192), BF16),
-        shape((192, 128), F32),
-        shape((16, 128), F32),
-        shape((384, 128), F32),
-    ]
-    made = pl.pallas_call(
-        exchange_kernel,
-        out_shape=outs,
+    flows = pl.pallas_call(
+        kernel,
+        out_shape=shape((512, 128), F32),
         in_specs=[pl.BlockSpec(memory_space=pltpu.HBM)] * 7,
-        out_specs=[vmem] * 7,
+        out_specs=vmem,
         scratch_shapes=[
+            pltpu.VMEM((10, 64, 128), BF16),
+            pltpu.VMEM((256, 48), BF16),
+            pltpu.VMEM((192, 768), BF16),
+            pltpu.VMEM((48, 192), BF16),
+            pltpu.VMEM((192, 128), F32),
+            pltpu.VMEM((384, 128), F32),
+            pltpu.VMEM((1024, 128), F32),
+            pltpu.VMEM((256, 36 * 128), BF16),
+            pltpu.VMEM((192, 34 * 128), BF16),
+            pltpu.VMEM((48, 34 * 128), F32),
             pltpu.VMEM((3, 3, 32), BF16),
             pltpu.VMEM((1, 32), F32),
             pltpu.VMEM((3, 3, 32, 32), BF16),
@@ -371,24 +438,11 @@
             pltpu.VMEM((1152, 256), BF16),
             pltpu.VMEM((1088, 256), BF16),
             pltpu.SemaphoreType.DMA((7,)),
-            pltpu.SemaphoreType.DMA((8,)),
-            pltpu.SemaphoreType.DMA((8,)),
+            pltpu.SemaphoreType.DMA((9,)),
+            pltpu.SemaphoreType.DMA((9,)),
         ],
         compiler_params=pltpu.CompilerParams(collective_id=0, has_side_effects=True, vmem_limit_bytes=24 * 2**20),
     )(*args)
-    flows = pl.pallas_call(
-        yz_kernel,
-        out_shape=shape((512, 128), F32),
-        in_specs=[vmem] * 7,
-        out_specs=vmem,
-        scratch_shapes=[
-            pltpu.VMEM((1024, 128), F32),
-            pltpu.VMEM((256, 36 * 128), BF16),
-            pltpu.VMEM((192, 34 * 128), BF16),
-            pltpu.VMEM((48, 34 * 128), F32),
-        ],
-        compiler_params=pltpu.CompilerParams(vmem_limit_bytes=24 * 2**20),
-    )(*made)
     return flows.reshape(4, 4, 32, 128)
 
 

time: 21.5 us -> 18 us (0.84)
  the two profiles are of different devices: /device:TPU:7 before, /device:TPU:23 now
where the time goes in v2:
time: 18 us; the launch traced here: 17.9 us
  Pallas kernels  17.2 us (96%)
  local copies, waits for them, and re-layouts  0.71 us (4%)
    pallas_call x1, Pallas kernels, local(): pl.pallas_call(kernel, out_shape=shape((512, 128), F32), in_specs=[pl.Blo...  17.2 us
    unnamed x1, local copies, waits for them, and re-layouts  0.71 us

profile of v2, /device:TPU:23, one launch (start us, length us, event | category | flops | bytes accessed | tf_op | source)
XLA Modules:
  0.0 17.9 jit_solution(14804351227417052545)
XLA Ops:
  0.0 17.2 %shard_map.73 = f32[512,128]{1,0:T(8,128)S(1)} custom-call(bf16[4,32,128]{2,1,0:T(8,128)(2,1)} %img.1, bf16[3,3,32]{2,1,0:T(4,128)(2,1)} %bitcast.6, f32[1,32]{1,0:T(1,128)} %bitcast.7, bf16[3,3,32,32]{3,2,1,0:T(8,128)(2,1)} %k2.1, f32[1,32]{1,0:T(1,128)} %bitcast.8, bf16[3,3,3,32]{3,2,1,0:T(4,128)(2,1)} %k3.1, f32[1,3]{1,0:T(1,128)} %bitcast.9), custom_call_target="tpu_custom_call" | custom-call | tf_op jit(solution)/shard_map/pallas_call | solution.py:410
  17.2 0.7 %copy.9 = f32[4,4,32,128]{3,2,1,0:T(8,128)} copy(f32[4,4,32,128]{3,2,1,0:T(8,128)S(1)} %bitcast.5) | data formatting | bytes 524288

commit v3 on v2

--- a/solution.py
+++ b/solution.py
@@ -9,7 +9,7 @@
 F32 = jnp.float32
 BF16 = jnp.bfloat16
 
-SIDES = [(ds, dr) for ds in (1, -1, 0) for dr in (0, 1, -1) if ds or dr]
+SIDES = [(ds, dr) for ds in (1, -1, 0) for dr in (-1, 0, 1) if ds or dr]
 RUN = 32
 
 
@@ -41,28 +41,27 @@
     slabs = lax.axis_size("slab")
     rows = lax.axis_size("row")
     place = lax.rem(s, RUN)
-    wrap = place == RUN - 1
+    wrap = (place == RUN - 1) & (s < slabs - 1)
 
     def inside(ds, dr):
         return (s + ds >= 0) & (s + ds < slabs) & (r + dr >= 0) & (r + dr < rows)
 
-    def uneven(ds):
-        return wrap if ds == 0 else (wrap | (place == RUN - 2) if ds > 0 else wrap | (place == 0))
-
-    def first(ds, dr):
-        if ds == 0:
-            return (r ^ 1) < ((r + dr) ^ 1)
-        if ds > 0:
-            return jnp.bool_(False)
-        return jnp.bool_(True)
+    def greets(ds):
+        return wrap | (place == 0) if ds < 0 else jnp.bool_(False)
+
+    def greeted_by(ds):
+        return wrap | ((place == RUN - 2) & (s < slabs - 2)) if ds > 0 else jnp.bool_(False)
+
+    def aside(ds):
+        return wrap if ds == 0 else jnp.bool_(False)
 
     barrier = pltpu.get_barrier_semaphore()
     greeted = jnp.int32(0)
     for ds, dr in SIDES:
-        greeted += (inside(ds, dr) & ~(uneven(ds) & first(ds, dr))).astype(jnp.int32)
+        greeted += (inside(ds, dr) & ~greets(ds) & ~aside(ds)).astype(jnp.int32)
 
     def greet(ds, dr):
-        @pl.when(inside(ds, dr) & ~(uneven(ds) & ~first(ds, dr)))
+        @pl.when(inside(ds, dr) & ~greeted_by(ds) & ~aside(ds))
         def _():
             pl.semaphore_signal(barrier, inc=1, device_id=(s + ds, r + dr), device_id_type=MESH)
 
@@ -88,7 +87,6 @@
         device_id_type=MESH,
     )
     head = (place == 0) & (s > 0)
-    tail = wrap & (s < slabs - 1)
 
     def meet_and_send():
         @pl.when(greeted > 0)
@@ -97,7 +95,7 @@
 
         for ds, dr in SIDES:
 
-            @pl.when(inside(ds, dr) & ~(uneven(ds) & first(ds, dr)))
+            @pl.when(inside(ds, dr) & ~greets(ds) & ~aside(ds))
             def _():
                 copies[ds, dr].start()
 
@@ -106,7 +104,7 @@
         def _():
             copies[-ds, -dr].wait_recv()
 
-        @pl.when(inside(ds, dr) & uneven(ds) & first(ds, dr))
+        @pl.when(inside(ds, dr) & greets(ds))
         def _():
             copies[ds, dr].start()
 
@@ -141,12 +139,14 @@
         z0, z1 = {-1: (0, 3), 0: (3, 7), 1: (7, 10)}[ds]
         y0, y1 = {-1: (0, 16), 0: (16, 48), 1: (48, 64)}[dr]
 
-        @pl.when(~inside(ds, dr) & ~(tail if ds == 1 else jnp.bool_(False)))
+        @pl.when(~inside(ds, dr) & ~(wrap if ds == 1 else jnp.bool_(False)))
         def _():
             ext[z0:z1, y0:y1, :] = jnp.zeros((z1 - z0, y1 - y0, 128), BF16)
 
     for z in range(10, 16):
         imt[pl.ds(z, 64, stride=16), :] = jnp.ones((64, 128), F32)
+    for z in range(10):
+        imt[pl.ds(z, 64, stride=16), :] = jnp.zeros((64, 128), F32)
     for load in loads:
         load.wait()
 
@@ -185,22 +185,31 @@
     )
     w1z[...] = flat.T[:, :48].astype(BF16)
 
-    z_of = s * 4 + (iota((32, 256), 1) >> 5)
-    in_two = (z_of >= 2) & (z_of < 4 * slabs + 2)
-    part = iota((32, 256), 1) >> 5
-    wide = dot(k2v[...].reshape(288, 32), spread(32, 256))
-    for b in range(3):
-        for o in range(6):
-            block = jnp.zeros((32, 256), F32)
-            for a in range(3):
-                n = (3 * a + b) * 32
-                block = jnp.where(part == o + a, wide[n : n + 32], block)
-            w2x[o * 32 : o * 32 + 32, b * 256 : b * 256 + 256] = block.astype(BF16)
-            w2z[o * 32 : o * 32 + 32, b * 256 : b * 256 + 256] = jnp.where(in_two, block, 0.0).astype(BF16)
+    lane = iota((32, 480), 1)
+    wide = sum(
+        dot(
+            k2v[:, b].reshape(96, 32),
+            ((lane >= 160 * b) & (lane < 160 * b + 160) & ((lane & 31) == iota((32, 480), 0))).astype(BF16),
+        )
+        for b in range(3)
+    )
+    part = (lane - jnp.where(lane >= 320, 320, jnp.where(lane >= 160, 160, 0))) >> 5
+
+    def in_two(skip):
+        z = s * 4 - 2 + skip + part
+        return (z >= 0) & (z < 4 * slabs)
+
+    for o in range(3):
+        block = jnp.zeros((32, 480), F32)
+        for a in range(3):
+            block = jnp.where(part == o + a, wide[a * 32 : a * 32 + 32], block)
+        w2x[o * 32 : o * 32 + 32, :] = block.astype(BF16)
+        for h, skip in ((0, 0), (1, 3)):
+            w2z[h, o * 32 : o * 32 + 32, :] = jnp.where(in_two(skip), block, 0.0).astype(BF16)
     column = jnp.sum(
         jnp.where(iota((32, 32), 0) == iota((32, 32), 1), jnp.broadcast_to(b2v[...], (32, 32)), 0.0), axis=1, keepdims=True
     )
-    for o in range(6):
+    for o in range(3):
         b2c[o * 32 : o * 32 + 32, :] = jnp.broadcast_to(column, (32, 128))
 
     group = iota((48, 32), 0) >> 2
@@ -232,13 +241,20 @@
     def _():
         meet_and_send()
 
+    @pl.when(wrap)
+    def _():
+        arrive(-1, 0)
+        for dr in (1, -1):
+
+            @pl.when(inside(0, dr))
+            def _():
+                copies[0, dr].start()
+
+        arrive(-1, 1)
+        arrive(-1, -1)
+
     arrive(0, 1)
     arrive(0, -1)
-
-    @pl.when(wrap)
-    def _():
-        for dr in (0, 1, -1):
-            arrive(-1, dr)
 
     lane = iota((64, 128), 1)
     for z in range(4):
@@ -275,10 +291,10 @@
             def _():
                 ref[1088:] = jnp.zeros((64, 256), BF16)
 
-        for first in (0, 6, 12, 18, 24, 28):
-            at = first * 32
-            rhs = jnp.concatenate([ref[at : at + 256] for ref in (h1l, h1c, h1r)], axis=0)
-            h2x[at : at + 192] = jnp.maximum(dot(w2x[...], rhs) + bias_two, 0.0).astype(BF16)
+        for start in (0, 3, 6, 9, 12, 15, 18, 21, 24, 27, 30, 31):
+            at = start * 32
+            rhs = jnp.concatenate([ref[at : at + 160] for ref in (h1l, h1c, h1r)], axis=0)
+            h2x[at : at + 96] = jnp.maximum(dot(w2x[...], rhs) + bias_two, 0.0).astype(BF16)
 
         @pl.when(r == 0)
         def _():
@@ -313,71 +329,79 @@
         def _():
             arrive(-1, dr)
 
+    top = jnp.where(r == 0, 0.0, 1.0)
+    bottom = jnp.where(r == rows - 1, 0.0, 1.0)
+
+    part_one = ((0, 96), (96, 256))
+
+    def one(h, j):
+        lo, hi = part_one[h]
+        rhs = jnp.concatenate([imt[(j + i + 13) * 16 : (j + i + 16) * 16, :].astype(BF16) for i in range(2)], axis=1)
+        hidden = jnp.maximum(dot(w1z[lo:hi], rhs), 0.0)
+        if j == 0:
+            hidden = hidden * top
+        if j == 34:
+            hidden = hidden * bottom
+        g1[lo:hi, j * 128 : j * 128 + 256] = hidden.astype(BF16)
+
+    def two(h, j):
+        at = 96 * h
+        rhs = jnp.concatenate([g1[at : at + 160, (j + b) * 128 : (j + b) * 128 + 256] for b in range(3)], axis=0)
+        hidden = jnp.maximum(dot(w2z[h], rhs) + bias_two, 0.0)
+        if j == 0:
+            hidden = jnp.concatenate([hidden[:, :128] * top, hidden[:, 128:]], axis=1)
+        if j == 32:
+            hidden = jnp.concatenate([hidden[:, :128], hidden[:, 128:] * bottom], axis=1)
+        g2[at : at + 96, j * 128 : j * 128 + 256] = hidden.astype(BF16)
+
+    def three(j):
+        p3[:, j * 128 : j * 128 + 256] = dot(w3z[...], g2[:, j * 128 : j * 128 + 256])
+
+    def finish(y):
+        total = sum(p3[16 * b : 16 * b + 16, (y + b) * 128 : (y + b) * 128 + 128] for b in range(3))
+        flows = total * scale_yz + bias_yz
+        out[pl.ds(y, 8, stride=32), :] = flows[:8]
+        out[pl.ds(384 + y, 4, stride=32), :] = flows[8:12]
+
     turn(3, 7, 0, 64)
     arrive_high(0)
     arrive_high(-1)
 
-    @pl.when(tail)
+    @pl.when(wrap)
     def _():
         broad.wait_recv()
 
     turn(7, 10, 0, 48)
+    for k in range(16):
+        one(1, 2 * k)
+    for k in range(15):
+        two(1, 2 * k)
     arrive_low(0)
     arrive_low(-1)
     arrive_head(0)
     arrive_head(-1)
     turn(0, 3, 0, 48)
-
-    top = jnp.where(r == 0, 0.0, 1.0)
-    bottom = jnp.where(r == rows - 1, 0.0, 1.0)
-
-    def one(j):
-        rhs = jnp.concatenate([imt[(j + h + 13) * 16 : (j + h + 16) * 16, :].astype(BF16) for h in range(2)], axis=1)
-        hidden = jnp.maximum(dot(w1z[...], rhs), 0.0)
-        if j == 0:
-            hidden = hidden * top
-        if j == 34:
-            hidden = hidden * bottom
-        g1[:, j * 128 : j * 128 + 256] = hidden.astype(BF16)
-
-    def two(j):
-        rhs = jnp.concatenate([g1[:, (j + b) * 128 : (j + b) * 128 + 256] for b in range(3)], axis=0)
-        hidden = jnp.maximum(dot(w2z[...], rhs) + bias_two, 0.0)
-        if j == 0:
-            hidden = jnp.concatenate([hidden[:, :128] * top, hidden[:, 128:]], axis=1)
-        if j == 32:
-            hidden = jnp.concatenate([hidden[:, :128], hidden[:, 128:] * bottom], axis=1)
-        g2[:, j * 128 : j * 128 + 256] = hidden.astype(BF16)
-
-    def three(j):
-        p3[:, j * 128 : j * 128 + 256] = dot(w3z[...], g2[:, j * 128 : j * 128 + 256])
-
-    def finish(y):
-        total = sum(p3[16 * b : 16 * b + 16, (y + b) * 128 : (y + b) * 128 + 128] for b in range(3))
-        flows = total * scale_yz + bias_yz
-        out[pl.ds(y, 8, stride=32), :] = flows[:8]
-        out[pl.ds(384 + y, 4, stride=32), :] = flows[8:12]
-
     for k in range(16):
-        one(2 * k)
+        one(0, 2 * k)
     for k in range(15):
-        two(2 * k)
-    for k in range(15):
-        three(2 * k)
-    for y in range(28):
-        finish(y)
+        two(0, 2 * k)
     arrive_high(1)
-    turn(7, 10, 48, 64)
     arrive_low(1)
     arrive_head(1)
+
+    turn(7, 10, 48, 64)
     turn(0, 3, 48, 64)
-    for k in range(16, 18):
-        one(2 * k)
-    for k in range(15, 17):
-        two(2 * k)
-    for k in range(15, 17):
+    for h in (1, 0):
+        for k in range(16, 18):
+            one(h, 2 * k)
+    for k in range(8):
         three(2 * k)
-    for y in range(28, 32):
+    for h in (1, 0):
+        for k in range(15, 17):
+            two(h, 2 * k)
+    for k in range(8, 17):
+        three(2 * k)
+    for y in range(32):
         finish(y)
     out[128:256, :] = out[128:256, :] + xyp[:128]
     out[256:384, :] = xyp[128:256]
@@ -415,9 +439,9 @@
         scratch_shapes=[
             pltpu.VMEM((10, 64, 128), BF16),
             pltpu.VMEM((256, 48), BF16),
-            pltpu.VMEM((192, 768), BF16),
+            pltpu.VMEM((2, 96, 480), BF16),
             pltpu.VMEM((48, 192), BF16),
-            pltpu.VMEM((192, 128), F32),
+            pltpu.VMEM((96, 128), F32),
             pltpu.VMEM((384, 128), F32),
             pltpu.VMEM((1024, 128), F32),
             pltpu.VMEM((256, 36 * 128), BF16),
@@ -430,7 +454,7 @@
             pltpu.VMEM((3, 3, 3, 32), BF16),
             pltpu.VMEM((1, 3), F32),
             pltpu.VMEM((512, 128), BF16),
-            pltpu.VMEM((192, 768), BF16),
+            pltpu.VMEM((96, 480), BF16),
             pltpu.VMEM((48, 192), BF16),
             pltpu.VMEM((3, 64, 512), BF16),
             pltpu.VMEM((1152, 256), BF16),

time: 18 us -> 17 us (0.944)
  the two profiles are of different devices: /device:TPU:23 before, /device:TPU:489 now
where the time goes in v3:
time: 17 us; the launch traced here: 16.8 us
  Pallas kernels  16.1 us (95%)
  local copies, waits for them, and re-layouts  0.71 us (4%)
    pallas_call x1, Pallas kernels, local(): pl.pallas_call(kernel, out_shape=shape((512, 128), F32), in_specs=[pl.Blo...  16.1 us
    unnamed x1, local copies, waits for them, and re-layouts  0.71 us

profile of v3, /device:TPU:489, one launch (start us, length us, event | category | flops | bytes accessed | tf_op | source)
XLA Modules:
  0.0 16.8 jit_solution(3455369211954494001)
XLA Ops:
  0.0 16.1 %shard_map.73 = f32[512,128]{1,0:T(8,128)S(1)} custom-call(bf16[4,32,128]{2,1,0:T(8,128)(2,1)} %img.1, bf16[3,3,32]{2,1,0:T(4,128)(2,1)} %bitcast.6, f32[1,32]{1,0:T(1,128)} %bitcast.7, bf16[3,3,32,32]{3,2,1,0:T(8,128)(2,1)} %k2.1, f32[1,32]{1,0:T(1,128)} %bitcast.8, bf16[3,3,3,32]{3,2,1,0:T(4,128)(2,1)} %k3.1, f32[1,3]{1,0:T(1,128)} %bitcast.9), custom_call_target="tpu_custom_call" | custom-call | tf_op jit(solution)/shard_map/pallas_call | solution.py:434
  16.1 0.7 %copy.9 = f32[4,4,32,128]{3,2,1,0:T(8,128)} copy(f32[4,4,32,128]{3,2,1,0:T(8,128)S(1)} %bitcast.5) | data formatting | bytes 524288

commit v4 on v3

--- a/solution.py
+++ b/solution.py
@@ -46,11 +46,14 @@
     def inside(ds, dr):
         return (s + ds >= 0) & (s + ds < slabs) & (r + dr >= 0) & (r + dr < rows)
 
-    def greets(ds):
-        return wrap | (place == 0) if ds < 0 else jnp.bool_(False)
+    corner = (s == 0) & (r == 0)
+
+    def greets(ds, dr):
+        to_corner = (s + ds == 0) & (r + dr == 0)
+        return (wrap | (place == 0) | to_corner) if ds < 0 else to_corner
 
     def greeted_by(ds):
-        return wrap | ((place == RUN - 2) & (s < slabs - 2)) if ds > 0 else jnp.bool_(False)
+        return (wrap | ((place == RUN - 2) & (s < slabs - 2)) | corner) if ds > 0 else corner
 
     def aside(ds):
         return wrap if ds == 0 else jnp.bool_(False)
@@ -58,7 +61,7 @@
     barrier = pltpu.get_barrier_semaphore()
     greeted = jnp.int32(0)
     for ds, dr in SIDES:
-        greeted += (inside(ds, dr) & ~greets(ds) & ~aside(ds)).astype(jnp.int32)
+        greeted += (inside(ds, dr) & ~greets(ds, dr) & ~aside(ds)).astype(jnp.int32)
 
     def greet(ds, dr):
         @pl.when(inside(ds, dr) & ~greeted_by(ds) & ~aside(ds))
@@ -95,7 +98,7 @@
 
         for ds, dr in SIDES:
 
-            @pl.when(inside(ds, dr) & ~greets(ds) & ~aside(ds))
+            @pl.when(inside(ds, dr) & ~greets(ds, dr) & ~aside(ds))
             def _():
                 copies[ds, dr].start()
 
@@ -104,7 +107,7 @@
         def _():
             copies[-ds, -dr].wait_recv()
 
-        @pl.when(inside(ds, dr) & greets(ds))
+        @pl.when(inside(ds, dr) & greets(ds, dr))
         def _():
             copies[ds, dr].start()
 
@@ -118,7 +121,7 @@
     greet(0, 1)
     greet(0, -1)
 
-    @pl.when(wrap)
+    @pl.when(wrap | corner)
     def _():
         meet_and_send()
 
@@ -237,7 +240,7 @@
     bias_xy = jnp.where(kind == 0, 0.5 * (flow[0] + flow[1]), jnp.where(kind == 1, flow[1], flow[2]))
     scale_xy = jnp.where(kind == 1, 1.0, 0.5)
 
-    @pl.when(~wrap)
+    @pl.when(~wrap & ~corner)
     def _():
         meet_and_send()
 
@@ -253,23 +256,63 @@
         arrive(-1, 1)
         arrive(-1, -1)
 
-    arrive(0, 1)
     arrive(0, -1)
 
-    lane = iota((64, 128), 1)
-    for z in range(4):
-        plane = ext[3 + z].astype(F32)
-        at = pl.ds(z * 128, 128)
-        imx[0, :, at] = jnp.where(lane == 0, 0.0, pltpu.roll(plane, 1, 1)).astype(BF16)
-        imx[1, :, at] = plane.astype(BF16)
-        imx[2, :, at] = jnp.where(lane == 127, 0.0, pltpu.roll(plane, 127, 1)).astype(BF16)
+    bias_two = jnp.concatenate([b2c[...]] * 2, axis=1)
+
+    def turn(z0, z1, y0, y1):
+        for z in range(z0, z1):
+            imt[pl.ds(16 * y0 + z, y1 - y0, stride=16), :] = ext[z, y0:y1, :].astype(F32)
+
+    def arrive_high(dr):
+        @pl.when(~wrap)
+        def _():
+            arrive(1, dr)
+
+    def arrive_low(dr):
+        @pl.when(~wrap & ~head)
+        def _():
+            arrive(-1, dr)
+
+    top = jnp.where(r == 0, 0.0, 1.0)
+    bottom = jnp.where(r == rows - 1, 0.0, 1.0)
+
+    part_one = ((0, 96), (96, 256))
+
+    def one(h, j):
+        lo, hi = part_one[h]
+        rhs = jnp.concatenate([imt[(j + i + 13) * 16 : (j + i + 16) * 16, :].astype(BF16) for i in range(2)], axis=1)
+        hidden = jnp.maximum(dot(w1z[lo:hi], rhs), 0.0)
+        if j == 0:
+            hidden = hidden * top
+        if j == 34:
+            hidden = hidden * bottom
+        g1[lo:hi, j * 128 : j * 128 + 256] = hidden.astype(BF16)
+
+    def two(h, j):
+        at = 96 * h
+        rhs = jnp.concatenate([g1[at : at + 160, (j + b) * 128 : (j + b) * 128 + 256] for b in range(3)], axis=0)
+        hidden = jnp.maximum(dot(w2z[h], rhs) + bias_two, 0.0)
+        if j == 0:
+            hidden = jnp.concatenate([hidden[:, :128] * top, hidden[:, 128:]], axis=1)
+        if j == 32:
+            hidden = jnp.concatenate([hidden[:, :128], hidden[:, 128:] * bottom], axis=1)
+        g2[at : at + 96, j * 128 : j * 128 + 256] = hidden.astype(BF16)
+
+    def three(j):
+        p3[:, j * 128 : j * 128 + 256] = dot(w3z[...], g2[:, j * 128 : j * 128 + 256])
+
+    def finish(y):
+        total = sum(p3[16 * b : 16 * b + 16, (y + b) * 128 : (y + b) * 128 + 128] for b in range(3))
+        flows = total * scale_yz + bias_yz
+        out[pl.ds(y, 8, stride=32), :] = flows[:8]
+        out[pl.ds(384 + y, 4, stride=32), :] = flows[8:12]
 
     def shifted(values, by):
         edge = iota((values.shape[0], 128), 1) == (0 if by > 0 else 127)
         halves = [jnp.where(edge, 0.0, pltpu.roll(values[:, h : h + 128], by % 128, 1)) for h in (0, 128)]
         return jnp.concatenate(halves, axis=1)
 
-    bias_two = jnp.concatenate([b2c[...]] * 2, axis=1)
 
     def pair(t, carry):
         cols = pl.ds(pl.multiple_of(t * 256, 256), 256)
@@ -313,69 +356,48 @@
                     xyp[pl.ds((4 * f + 2 * t + h) * 32 + 4 * k, 4), :] = flows[4 * f : 4 * f + 4]
         return carry
 
-    lax.fori_loop(0, 2, pair, 0)
-
-    def turn(z0, z1, y0, y1):
-        for z in range(z0, z1):
-            imt[pl.ds(16 * y0 + z, y1 - y0, stride=16), :] = ext[z, y0:y1, :].astype(F32)
-
-    def arrive_high(dr):
-        @pl.when(~wrap)
-        def _():
-            arrive(1, dr)
-
-    def arrive_low(dr):
-        @pl.when(~wrap & ~head)
-        def _():
-            arrive(-1, dr)
-
-    top = jnp.where(r == 0, 0.0, 1.0)
-    bottom = jnp.where(r == rows - 1, 0.0, 1.0)
-
-    part_one = ((0, 96), (96, 256))
-
-    def one(h, j):
-        lo, hi = part_one[h]
-        rhs = jnp.concatenate([imt[(j + i + 13) * 16 : (j + i + 16) * 16, :].astype(BF16) for i in range(2)], axis=1)
-        hidden = jnp.maximum(dot(w1z[lo:hi], rhs), 0.0)
-        if j == 0:
-            hidden = hidden * top
-        if j == 34:
-            hidden = hidden * bottom
-        g1[lo:hi, j * 128 : j * 128 + 256] = hidden.astype(BF16)
-
-    def two(h, j):
-        at = 96 * h
-        rhs = jnp.concatenate([g1[at : at + 160, (j + b) * 128 : (j + b) * 128 + 256] for b in range(3)], axis=0)
-        hidden = jnp.maximum(dot(w2z[h], rhs) + bias_two, 0.0)
-        if j == 0:
-            hidden = jnp.concatenate([hidden[:, :128] * top, hidden[:, 128:]], axis=1)
-        if j == 32:
-            hidden = jnp.concatenate([hidden[:, :128], hidden[:, 128:] * bottom], axis=1)
-        g2[at : at + 96, j * 128 : j * 128 + 256] = hidden.astype(BF16)
-
-    def three(j):
-        p3[:, j * 128 : j * 128 + 256] = dot(w3z[...], g2[:, j * 128 : j * 128 + 256])
-
-    def finish(y):
-        total = sum(p3[16 * b : 16 * b + 16, (y + b) * 128 : (y + b) * 128 + 128] for b in range(3))
-        flows = total * scale_yz + bias_yz
-        out[pl.ds(y, 8, stride=32), :] = flows[:8]
-        out[pl.ds(384 + y, 4, stride=32), :] = flows[8:12]
-
-    turn(3, 7, 0, 64)
-    arrive_high(0)
-    arrive_high(-1)
-
-    @pl.when(wrap)
-    def _():
-        broad.wait_recv()
-
-    turn(7, 10, 0, 48)
-    for k in range(16):
-        one(1, 2 * k)
-    for k in range(15):
-        two(1, 2 * k)
+    def along_x():
+        arrive(0, 1)
+        lane = iota((64, 128), 1)
+        for z in range(4):
+            plane = ext[3 + z].astype(F32)
+            at = pl.ds(z * 128, 128)
+            imx[0, :, at] = jnp.where(lane == 0, 0.0, pltpu.roll(plane, 1, 1)).astype(BF16)
+            imx[1, :, at] = plane.astype(BF16)
+            imx[2, :, at] = jnp.where(lane == 127, 0.0, pltpu.roll(plane, 127, 1)).astype(BF16)
+
+        lax.fori_loop(0, 2, pair, 0)
+
+    def high_half():
+        arrive_high(0)
+        arrive_high(-1)
+
+        @pl.when(wrap)
+        def _():
+            broad.wait_recv()
+
+        turn(7, 10, 0, 48)
+        for k in range(16):
+            one(1, 2 * k)
+        for k in range(15):
+            two(1, 2 * k)
+
+    turn(3, 7, 0, 48)
+    ahead = (r == 1) & (s > 0) & (place != RUN - 2)
+
+    def either(t, carry):
+        @pl.when((t == 0) ^ ahead)
+        def _():
+            along_x()
+
+        @pl.when((t == 1) ^ ahead)
+        def _():
+            high_half()
+
+        return carry
+
+    lax.fori_loop(0, 2, either, 0)
+
     arrive_low(0)
     arrive_low(-1)
     arrive_head(0)
@@ -385,26 +407,29 @@
         one(0, 2 * k)
     for k in range(15):
         two(0, 2 * k)
+    for k in range(15):
+        three(2 * k)
     arrive_high(1)
     arrive_low(1)
     arrive_head(1)
 
-    turn(7, 10, 48, 64)
-    turn(0, 3, 48, 64)
+    turn(0, 10, 48, 64)
     for h in (1, 0):
         for k in range(16, 18):
             one(h, 2 * k)
-    for k in range(8):
-        three(2 * k)
+    for y in range(14):
+        finish(y)
     for h in (1, 0):
         for k in range(15, 17):
             two(h, 2 * k)
-    for k in range(8, 17):
+    for y in range(14, 28):
+        finish(y)
+    for k in range(15, 17):
         three(2 * k)
-    for y in range(32):
+    out[256:384, :] = xyp[128:256]
+    for y in range(28, 32):
         finish(y)
     out[128:256, :] = out[128:256, :] + xyp[:128]
-    out[256:384, :] = xyp[128:256]
     out[384:512, :] = out[384:512, :] + xyp[256:]
 
     for ds, dr in SIDES:

time: 17 us -> 16.8 us (0.988)
  the two profiles are of different devices: /device:TPU:489 before, /device:TPU:7 now
where the time goes in v4:
time: 16.8 us; the launch traced here: 16.7 us
  Pallas kernels  15.9 us (95%)
  local copies, waits for them, and re-layouts  0.71 us (4%)
    pallas_call x1, Pallas kernels, local(): pl.pallas_call(kernel, out_shape=shape((512, 128), F32), in_specs=[pl.Blo...  15.9 us
    unnamed x1, local copies, waits for them, and re-layouts  0.71 us

profile of v4, /device:TPU:7, one launch (start us, length us, event | category | flops | bytes accessed | tf_op | source)
XLA Modules:
  0.0 16.7 jit_solution(3084445523707973431)
XLA Ops:
  0.0 15.9 %shard_map.73 = f32[512,128]{1,0:T(8,128)S(1)} custom-call(bf16[4,32,128]{2,1,0:T(8,128)(2,1)} %img.1, bf16[3,3,32]{2,1,0:T(4,128)(2,1)} %bitcast.6, f32[1,32]{1,0:T(1,128)} %bitcast.7, bf16[3,3,32,32]{3,2,1,0:T(8,128)(2,1)} %k2.1, f32[1,32]{1,0:T(1,128)} %bitcast.8, bf16[3,3,3,32]{3,2,1,0:T(4,128)(2,1)} %k3.1, f32[1,3]{1,0:T(1,128)} %bitcast.9), custom_call_target="tpu_custom_call" | custom-call | tf_op jit(solution)/shard_map/pallas_call | solution.py:459
  16.0 0.7 %copy.9 = f32[4,4,32,128]{3,2,1,0:T(8,128)} copy(f32[4,4,32,128]{3,2,1,0:T(8,128)S(1)} %bitcast.5) | data formatting | bytes 524288

commit v5 on v4

--- a/solution.py
+++ b/solution.py
@@ -32,9 +32,9 @@
 def kernel(
     img, k1, b1, k2, b2, k3, b3,
     out,
-    ext, w1z, w2z, w3z, b2c, xyp, imt, g1, g2, p3,
+    ext, w1z, w2z, w3z, b2c, imt, g1, g2, p3,
     k1v, b1v, k2v, b2v, k3v, b3v, w1x, w2x, w3x, imx, h1c, h1l, h1r, h2x,
-    load_sem, send_sem, recv_sem,
+    load_sem, send_sem, recv_sem, go_sem,
 ):
     s = lax.axis_index("slab")
     r = lax.axis_index("row")
@@ -115,8 +115,6 @@
         @pl.when(head & inside(-1, dr))
         def _():
             copies[1, -dr].wait_recv()
-            if dr == 0:
-                broad.start()
 
     greet(0, 1)
     greet(0, -1)
@@ -124,6 +122,10 @@
     @pl.when(wrap | corner)
     def _():
         meet_and_send()
+
+    @pl.when(wrap)
+    def _():
+        pl.semaphore_signal(go_sem, inc=1, device_id=(s + 1, r), device_id_type=MESH)
 
     for ds in (1, -1):
         for dr in (0, 1, -1):
@@ -235,7 +237,7 @@
 
     kind = iota((16, 128), 0) >> 2
     flow = [jnp.broadcast_to(b3v[0:1, f : f + 1], (16, 128)) for f in range(3)]
-    bias_yz = jnp.where(kind == 0, flow[0], 0.0)
+    out[0:128, :] = jnp.broadcast_to(b3v[0:1, 0:1], (128, 128))
     scale_yz = jnp.where(kind == 0, 1.0, 0.5)
     bias_xy = jnp.where(kind == 0, 0.5 * (flow[0] + flow[1]), jnp.where(kind == 1, flow[1], flow[2]))
     scale_xy = jnp.where(kind == 1, 1.0, 0.5)
@@ -304,9 +306,9 @@
 
     def finish(y):
         total = sum(p3[16 * b : 16 * b + 16, (y + b) * 128 : (y + b) * 128 + 128] for b in range(3))
-        flows = total * scale_yz + bias_yz
-        out[pl.ds(y, 8, stride=32), :] = flows[:8]
-        out[pl.ds(384 + y, 4, stride=32), :] = flows[8:12]
+        flows = total * scale_yz
+        for lo, hi, at in ((0, 8, pl.ds(y, 8, stride=32)), (8, 12, pl.ds(384 + y, 4, stride=32))):
+            out[at, :] = out[at, :] + flows[lo:hi]
 
     def shifted(values, by):
         edge = iota((values.shape[0], 128), 1) == (0 if by > 0 else 127)
@@ -353,7 +355,7 @@
             for h in range(2):
                 flows = total[:, 128 * h : 128 * h + 128] * scale_xy + bias_xy
                 for f in range(3):
-                    xyp[pl.ds((4 * f + 2 * t + h) * 32 + 4 * k, 4), :] = flows[4 * f : 4 * f + 4]
+                    out[pl.ds((4 * f + 4 + 2 * t + h) * 32 + 4 * k, 4), :] = flows[4 * f : 4 * f + 4]
         return carry
 
     def along_x():
@@ -398,6 +400,17 @@
 
     lax.fori_loop(0, 2, either, 0)
 
+    @pl.when(head)
+    def _():
+        pl.semaphore_wait(go_sem, 1)
+        broad.start()
+
+    arrive_high(1)
+    turn(3, 10, 48, 64)
+    for k in range(16, 18):
+        one(1, 2 * k)
+    for k in range(15, 17):
+        two(1, 2 * k)
     arrive_low(0)
     arrive_low(-1)
     arrive_head(0)
@@ -409,28 +422,22 @@
         two(0, 2 * k)
     for k in range(15):
         three(2 * k)
-    arrive_high(1)
+        if k >= 3:
+            finish(2 * k - 6)
+            finish(2 * k - 5)
     arrive_low(1)
     arrive_head(1)
-
-    turn(0, 10, 48, 64)
-    for h in (1, 0):
-        for k in range(16, 18):
-            one(h, 2 * k)
-    for y in range(14):
-        finish(y)
-    for h in (1, 0):
-        for k in range(15, 17):
-            two(h, 2 * k)
-    for y in range(14, 28):
+    turn(0, 3, 48, 64)
+    for k in range(16, 18):
+        one(0, 2 * k)
+    for k in range(15, 17):
+        two(0, 2 * k)
+    for y in range(24, 28):
         finish(y)
     for k in range(15, 17):
         three(2 * k)
-    out[256:384, :] = xyp[128:256]
     for y in range(28, 32):
         finish(y)
-    out[128:256, :] = out[128:256, :] + xyp[:128]
-    out[384:512, :] = out[384:512, :] + xyp[256:]
 
     for ds, dr in SIDES:
 
@@ -467,7 +474,6 @@
             pltpu.VMEM((2, 96, 480), BF16),
             pltpu.VMEM((48, 192), BF16),
             pltpu.VMEM((96, 128), F32),
-            pltpu.VMEM((384, 128), F32),
             pltpu.VMEM((1024, 128), F32),
             pltpu.VMEM((256, 36 * 128), BF16),
             pltpu.VMEM((192, 34 * 128), BF16),
@@ -489,6 +495,7 @@
             pltpu.SemaphoreType.DMA((7,)),
             pltpu.SemaphoreType.DMA((9,)),
             pltpu.SemaphoreType.DMA((9,)),
+            pltpu.SemaphoreType.REGULAR,
         ],
         compiler_params=pltpu.CompilerParams(collective_id=0, has_side_effects=True, vmem_limit_bytes=24 * 2**20),
     )(*args)

time: 16.8 us -> 16.6 us (0.988)
  no operation moved by 1% of the time
where the time goes in v5:
time: 16.6 us; the launch traced here: 16.5 us
  Pallas kernels  15.8 us (95%)
  local copies, waits for them, and re-layouts  0.71 us (4%)
    pallas_call x1, Pallas kernels, local(): pl.pallas_call(kernel, out_shape=shape((512, 128), F32), in_specs=[pl.Blo...  15.8 us
    unnamed x1, local copies, waits for them, and re-layouts  0.71 us

profile of v5, /device:TPU:7, one launch (start us, length us, event | category | flops | bytes accessed | tf_op | source)
XLA Modules:
  0.0 16.5 jit_solution(17715951385986699)
XLA Ops:
  0.0 15.8 %shard_map.73 = f32[512,128]{1,0:T(8,128)S(1)} custom-call(bf16[4,32,128]{2,1,0:T(8,128)(2,1)} %img.1, bf16[3,3,32]{2,1,0:T(4,128)(2,1)} %bitcast.6, f32[1,32]{1,0:T(1,128)} %bitcast.7, bf16[3,3,32,32]{3,2,1,0:T(8,128)(2,1)} %k2.1, f32[1,32]{1,0:T(1,128)} %bitcast.8, bf16[3,3,3,32]{3,2,1,0:T(4,128)(2,1)} %k3.1, f32[1,3]{1,0:T(1,128)} %bitcast.9), custom_call_target="tpu_custom_call" | custom-call | tf_op jit(solution)/shard_map/pallas_call | solution.py:466
  15.8 0.7 %copy.9 = f32[4,4,32,128]{3,2,1,0:T(8,128)} copy(f32[4,4,32,128]{3,2,1,0:T(8,128)S(1)} %bitcast.5) | data formatting | bytes 524288

commit v6 on v5

--- a/solution.py
+++ b/solution.py
@@ -233,7 +233,14 @@
         last = jnp.where(part3 == a, wide3[48 * a : 48 * a + 48], last)
     z_of = s * 4 + (iota((48, 192), 1) >> 5)
     w3x[...] = last.astype(BF16)
-    w3z[...] = jnp.where((z_of >= 1) & (z_of < 4 * slabs + 1), last, 0.0).astype(BF16)
+    in_three = (z_of >= 1) & (z_of < 4 * slabs + 1)
+    w3z[0] = jnp.where(in_three, last, 0.0)[:, :96].astype(BF16)
+    lane3 = (iota((48, 96), 1) >> 5) + 3
+    upper = jnp.zeros((48, 96), F32)
+    for a in range(3):
+        upper = jnp.where(lane3 - (iota((48, 96), 0) & 3) == a, wide3[48 * a : 48 * a + 48, :96], upper)
+    z_of = s * 4 + lane3
+    w3z[1] = jnp.where((z_of >= 1) & (z_of < 4 * slabs + 1), upper, 0.0).astype(BF16)
 
     kind = iota((16, 128), 0) >> 2
     flow = [jnp.broadcast_to(b3v[0:1, f : f + 1], (16, 128)) for f in range(3)]
@@ -301,8 +308,10 @@
             hidden = jnp.concatenate([hidden[:, :128], hidden[:, 128:] * bottom], axis=1)
         g2[at : at + 96, j * 128 : j * 128 + 256] = hidden.astype(BF16)
 
-    def three(j):
-        p3[:, j * 128 : j * 128 + 256] = dot(w3z[...], g2[:, j * 128 : j * 128 + 256])
+    def three(h, j):
+        at = slice(j * 128, j * 128 + 256)
+        terms = dot(w3z[h], g2[96 * h : 96 * h + 96, at])
+        p3[:, at] = terms if h else p3[:, at] + terms
 
     def finish(y):
         total = sum(p3[16 * b : 16 * b + 16, (y + b) * 128 : (y + b) * 128 + 128] for b in range(3))
@@ -383,6 +392,8 @@
             one(1, 2 * k)
         for k in range(15):
             two(1, 2 * k)
+        for k in range(15):
+            three(1, 2 * k)
 
     turn(3, 7, 0, 48)
     ahead = (r == 1) & (s > 0) & (place != RUN - 2)
@@ -411,6 +422,8 @@
         one(1, 2 * k)
     for k in range(15, 17):
         two(1, 2 * k)
+    for k in range(15, 17):
+        three(1, 2 * k)
     arrive_low(0)
     arrive_low(-1)
     arrive_head(0)
@@ -421,7 +434,7 @@
     for k in range(15):
         two(0, 2 * k)
     for k in range(15):
-        three(2 * k)
+        three(0, 2 * k)
         if k >= 3:
             finish(2 * k - 6)
             finish(2 * k - 5)
@@ -435,7 +448,7 @@
     for y in range(24, 28):
         finish(y)
     for k in range(15, 17):
-        three(2 * k)
+        three(0, 2 * k)
     for y in range(28, 32):
         finish(y)
 
@@ -472,7 +485,7 @@
             pltpu.VMEM((10, 64, 128), BF16),
             pltpu.VMEM((256, 48), BF16),
             pltpu.VMEM((2, 96, 480), BF16),
-            pltpu.VMEM((48, 192), BF16),
+            pltpu.VMEM((2, 48, 96), BF16),
             pltpu.VMEM((96, 128), F32),
             pltpu.VMEM((1024, 128), F32),
             pltpu.VMEM((256, 36 * 128), BF16),

time: 16.6 us -> 16.6 us (level)
  no operation moved by 1% of the time
where the time goes in v6:
time: 16.6 us; the launch traced here: 16.5 us
  Pallas kernels  15.8 us (95%)
  local copies, waits for them, and re-layouts  0.71 us (4%)
    pallas_call x1, Pallas kernels, local(): pl.pallas_call(kernel, out_shape=shape((512, 128), F32), in_specs=[pl.Blo...  15.8 us
    unnamed x1, local copies, waits for them, and re-layouts  0.71 us

profile of v6, /device:TPU:7, one launch (start us, length us, event | category | flops | bytes accessed | tf_op | source)
XLA Modules:
  0.0 16.5 jit_solution(18138430343322275232)
XLA Ops:
  0.0 15.8 %shard_map.73 = f32[512,128]{1,0:T(8,128)S(1)} custom-call(bf16[4,32,128]{2,1,0:T(8,128)(2,1)} %img.1, bf16[3,3,32]{2,1,0:T(4,128)(2,1)} %bitcast.6, f32[1,32]{1,0:T(1,128)} %bitcast.7, bf16[3,3,32,32]{3,2,1,0:T(8,128)(2,1)} %k2.1, f32[1,32]{1,0:T(1,128)} %bitcast.8, bf16[3,3,3,32]{3,2,1,0:T(4,128)(2,1)} %k3.1, f32[1,3]{1,0:T(1,128)} %bitcast.9), custom_call_target="tpu_custom_call" | custom-call | tf_op jit(solution)/shard_map/pallas_call | solution.py:479
  15.8 0.7 %copy.9 = f32[4,4,32,128]{3,2,1,0:T(8,128)} copy(f32[4,4,32,128]{3,2,1,0:T(8,128)S(1)} %bitcast.5) | data formatting | bytes 524288
